TPU v7x, 256 devices: a whole 4x4x8 slice. The times are simulated.
256 devices in a mesh: dp: 4 (over x), expert: 64 (over z, y, core).
Axes of the slice: x: 4, y: 4, z: 8, core: 2. Of those that a mesh axis runs over, the one named last changes fastest.
Arguments:
- stream_rows: bfloat16 [32768, 2880], P(('dp', 'expert')), may hold values from -6 to 6
- query_rows: bfloat16 [32768, 2048], P(('dp', 'expert')), may hold values from -150 to 150
- key_value_rows: bfloat16 [32768, 512], P(('dp', 'expert')), may hold values from -12 to 12
- destination: int32 [32768], P(('dp', 'expert')), may hold values from 0 to 32767, as said below
- lengths: int32 [64, 3], P('expert'), may hold values from 1 to 256, 512 in all within a row
- out_weight: bfloat16 [2048, 2880], P(None, 'dp'), may hold values from -0.125 to 0.125
- expert_index: int32 [64, 512, 4], P('expert', 'dp'), may hold values from 0 to 63, all different within a row
- router_weights: float32 [64, 512, 4], P('expert', 'dp'), may hold values from 0.1 to 0.6
- gate_up: bfloat16 [64, 2880, 2880], P('expert', None, 'dp'), may hold values from -0.109375 to 0.109375
- down_weight: bfloat16 [64, 1440, 2880], P('expert', 'dp'), may hold values from -0.15625 to 0.15625
Outputs:
- scored: bfloat16 [64, 512, 2880], P('expert', 'dp')
Inputs may be any that keep to these rules, and one draw needn't show every extreme that they name: destination is a permutation of the 32768 scorer rows. Generator block b of 128 rows (rows b * 128 onward, b = p * 64 + e for dp index p and expert index e) sends exactly 2 rows to every pack, all to positions p * 128 to (p + 1) * 128 - 1 of that pack.
All inputs are finite; a program needn't handle non-finite values.
Results may differ from a plain program's by a relative error of at most 0.012.
Values may be sent and summed in bfloat16 or wider, within the bound.
A program may use at most 128 MiB of HBM per device.

v0:
```python
import functools

import jax
import jax.numpy as jnp
from jax import lax
from jax.experimental import pallas as pl
from jax.experimental.pallas import tpu as pltpu
from jax.sharding import PartitionSpec as P

HEADS = 32
KV_HEADS = 4
HEAD_DIM = 64
TOPK = 4


masked_score = -1e30
norm_eps = 1e-05
f32 = jnp.float32
bf16 = jnp.bfloat16


def segment_number(seg_ends, positions):
    return jnp.sum((positions[:, None] >= seg_ends[None, :]).astype(jnp.int32), axis=1)


def pick(matrix, rows):
    return jnp.dot(matrix, rows, preferred_element_type=f32).astype(bf16)


def relation(index, cores, ys, zs):
    per = zs * cores
    chunk, rest = index // per, index % per
    dz = rest // cores
    return dz, (chunk + zs * ys - dz) % ys, rest % cores


def peer(expert, index, sign, cores, ys, zs):
    dz, dy, dc = relation(index, cores, ys, zs)
    z, y, c = expert // (ys * cores), (expert // cores) % ys, expert % cores
    z = (z + sign * dz + zs) % zs
    y = (y + sign * dy + ys) % ys
    c = (c + dc) % cores
    return (z * ys + y) * cores + c


def expert_kernel(
    grid,
    sent,
    dispatch,
    normed,
    residual,
    combine,
    own_in,
    near_in,
    own_out,
    result,
    raw_in,
    split_in,
    raw_out,
    out_buf,
    in_own,
    in_twin,
    x_buf,
    h_buf,
    own_part,
    part_send,
    part_recv,
    ret_recv,
    local_sem,
    weight_send,
    weight_recv,
    go_send,
    go_recv,
    twin_send,
    twin_recv,
    part_ssem,
    part_rsem,
    ret_send,
    ret_rsem,
):
    cores, ys, zs = grid
    x = lax.axis_index("dp")
    e = lax.axis_index("expert")
    odd = x % 2
    pair = (x + 1 - 2 * odd, e)
    twin = ((x + 2 * odd + 3) % 4, e)
    slabs, capacity, width = out_buf.shape
    per = slabs // 4
    rows = per * capacity
    columns = raw_in.shape[1]
    units = columns // 2
    padded = split_in.shape[1] // 2
    rest = columns - sent

    def remote(src, dst, ssem, rsem, device):
        return pltpu.make_async_remote_copy(
            src_ref=src, dst_ref=dst, send_sem=ssem, recv_sem=rsem, device_id=device, device_id_type=pl.DeviceIdType.MESH
        )

    weight_in = remote(
        own_in.at[pl.ds(sent, rest)], raw_in.at[1, pl.ds(sent, rest)], weight_send.at[0], weight_recv.at[0], pair
    )
    weight_out = remote(own_out, raw_out.at[1], weight_send.at[1], weight_recv.at[1], pair)
    weight_in.start()
    weight_out.start()
    load_own = pltpu.make_async_copy(own_in, raw_in.at[0], local_sem.at[0])
    load_near = pltpu.make_async_copy(near_in, raw_in.at[1, pl.ds(0, sent)], local_sem.at[1])
    load_out = pltpu.make_async_copy(own_out, raw_out.at[0], local_sem.at[2])
    load_own.start()
    load_near.start()
    load_out.start()

    def chunk_of(ref, c):
        return ref.at[pl.ds(c * per, per)]

    def send_dispatch(c, carry):
        picked = jnp.dot(dispatch[pl.ds(c * rows, rows), :], normed[...], preferred_element_type=f32)
        out_buf[pl.ds(c * per, per)] = picked.astype(bf16).reshape(per, capacity, width)

        def one(m, carry):
            index = c * per + m
            remote(
                out_buf.at[index], in_own.at[index], go_send.at[c], go_recv.at[c], (x, peer(e, index, 1, cores, ys, zs))
            ).start()
            return carry

        lax.fori_loop(jnp.where(c == 0, 1, 0), per, one, 0)
        return carry

    lax.fori_loop(0, 4, send_dispatch, 0)
    in_own[0] = out_buf[0]

    row = lax.broadcasted_iota(jnp.int32, (2 * padded, columns), 0)
    column = lax.broadcasted_iota(jnp.int32, (2 * padded, columns), 1)
    unit = jnp.where(row < padded, row, row - padded)
    wanted = jnp.where(unit < units, 2 * unit + jnp.where(row < padded, 0, 1), -1)
    part = (column == wanted).astype(f32).astype(bf16)

    def separate(k):
        for start in range(0, width, 768):
            cols = pl.ds(start, min(768, width - start))
            split_in[k, :, cols] = jnp.dot(part, raw_in[k, :, cols], preferred_element_type=f32).astype(bf16)

    load_own.wait()
    separate(0)

    def lead(ref, c):
        return ref.at[pl.ds(c * per, per)]

    def wait_own(c):
        @pl.when(c == 0)
        def _():
            view = in_own.at[pl.ds(1, per - 1)]
            remote(view, view, go_send.at[0], go_recv.at[0], twin).wait_recv()

        @pl.when(c > 0)
        def _():
            view = chunk_of(in_own, c)
            remote(view, view, go_send.at[c], go_recv.at[c], twin).wait_recv()

    def forward(c):
        return remote(chunk_of(in_own, c), chunk_of(in_twin, c), twin_send.at[c], twin_recv.at[c], twin)

    def partial(c):
        return remote(chunk_of(part_send, c), chunk_of(part_recv, c), part_ssem.at[c], part_rsem.at[c], twin)

    def wait_sent(ref, sems, c):
        @pl.when(c == 0)
        def _():
            view = ref.at[pl.ds(1, per - 1)]
            remote(view, view, sems.at[0], go_recv.at[0], twin).wait_send()

        @pl.when(c > 0)
        def _():
            view = chunk_of(ref, c)
            remote(view, view, sems.at[c], go_recv.at[c], twin).wait_send()

    def compute(c):
        x_buf[pl.ds(0, rows), :] = in_own[pl.ds(c * per, per)].reshape(rows, width)
        x_buf[pl.ds(rows, rows), :] = in_twin[pl.ds(c * per, per)].reshape(rows, width)

        def units_of(k, carry):
            projected = lax.dot_general(
                x_buf[...], split_in[k], (((1,), (1,)), ((), ())), preferred_element_type=f32
            )
            gate = projected[:, :padded]
            up = projected[:, padded:]
            hidden = (up + 1.0) * gate * (1.0 / (1.0 + jnp.exp(-1.702 * gate)))
            h_buf[k] = hidden.astype(bf16)
            return carry

        lax.fori_loop(0, 2, units_of, 0)
        for start in range(0, width, 768):
            size = min(768, width - start)
            cols = pl.ds(start, size)
            total = jnp.dot(h_buf[0, :, :units], raw_out[0, :, cols], preferred_element_type=f32)
            total += jnp.dot(h_buf[1, :, :units], raw_out[1, :, cols], preferred_element_type=f32)
            own_part[c, :, cols] = total[:rows]
            part_send[pl.ds(c * per, per), :, cols] = total[rows:].astype(bf16).reshape(per, capacity, size)

    def give_back(c):
        wait_sent(out_buf, go_send, c)
        total = own_part[c] + part_recv[pl.ds(c * per, per)].astype(f32).reshape(rows, width)
        out_buf[pl.ds(c * per, per)] = total.astype(bf16).reshape(per, capacity, width)

        def one(m, carry):
            index = c * per + m
            remote(
                out_buf.at[index], ret_recv.at[index], ret_send.at[c], ret_rsem.at[c], (x, peer(e, index, -1, cores, ys, zs))
            ).start()
            return carry

        lax.fori_loop(jnp.where(c == 0, 1, 0), per, one, 0)

    def step(t, carry):
        @pl.when(t < 4)
        def _():
            wait_own(t)
            forward(t).start()

        @pl.when(t == 1)
        def _():
            load_near.wait()
            load_out.wait()
            weight_in.wait()
            separate(1)
            weight_out.wait()

        @pl.when((t >= 1) & (t < 5))
        def _():
            forward(t - 1).wait_recv()
            compute(t - 1)
            partial(t - 1).start()

        @pl.when(t >= 2)
        def _():
            partial(t - 2).wait_recv()
            give_back(t - 2)

        return carry

    lax.fori_loop(0, 6, step, 0)
    ret_recv[0] = out_buf[0]

    def finish(c, carry):
        forward(c).wait_send()
        partial(c).wait_send()
        wait_sent(out_buf, ret_send, c)

        @pl.when(c == 0)
        def _():
            view = ret_recv.at[pl.ds(1, per - 1)]
            remote(view, view, go_send.at[0], ret_rsem.at[0], twin).wait_recv()

        @pl.when(c > 0)
        def _():
            view = chunk_of(ret_recv, c)
            remote(view, view, go_send.at[0], ret_rsem.at[c], twin).wait_recv()

        return carry

    lax.fori_loop(0, 4, finish, 0)
    for start in range(0, width, 768):
        size = min(768, width - start)
        cols = pl.ds(start, size)
        back = ret_recv[:, :, cols].reshape(slabs * capacity, size)
        mixed = jnp.dot(combine[0], back, preferred_element_type=f32)
        mixed += jnp.dot(combine[1], back, preferred_element_type=f32)
        result[:, cols] = (residual[:, cols] + mixed).astype(bf16)


def experts(grid, sent, dispatch, normed, residual, combine, own_in, near_in, own_out):
    slots, row_count = dispatch.shape
    width = normed.shape[1]
    columns = own_in.shape[0]
    units = columns // 2
    padded = -(-units // 128) * 128
    slabs = grid[0] * grid[1] * grid[2]
    capacity = slots // slabs
    rows = slots // 4
    vmem = pl.BlockSpec(memory_space=pltpu.VMEM)
    hbm = pl.BlockSpec(memory_space=pl.ANY)
    dma = pltpu.SemaphoreType.DMA
    buffer = pltpu.VMEM((slabs, capacity, width), bf16)
    return pl.pallas_call(
        functools.partial(expert_kernel, grid, sent),
        out_shape=jax.ShapeDtypeStruct((row_count, width), bf16),
        in_specs=[vmem, vmem, vmem, vmem, hbm, hbm, hbm],
        out_specs=vmem,
        scratch_shapes=[
            pltpu.VMEM((2, columns, width), bf16),
            pltpu.VMEM((2, 2 * padded, width), bf16),
            pltpu.VMEM((2, units, width), bf16),
            buffer,
            buffer,
            buffer,
            pltpu.VMEM((2 * rows, width), bf16),
            pltpu.VMEM((2, 2 * rows, padded), bf16),
            pltpu.VMEM((4, rows, width), f32),
            buffer,
            buffer,
            buffer,
            dma((3,)),
            dma((2,)),
            dma((2,)),
        ]
        + [dma((4,))] * 8,
        compiler_params=pltpu.CompilerParams(has_side_effects=True, vmem_limit_bytes=60 << 20),
        cost_estimate=pl.CostEstimate(flops=14 << 30, bytes_accessed=30 << 20, transcendentals=0),
        name="experts",
    )(dispatch, normed, residual, combine, own_in, near_in, own_out)


def on_device(
    stream_rows,
    query_rows,
    key_value_rows,
    destination,
    lengths,
    out_weight,
    expert_index,
    router_weights,
    gate_up,
    down_weight,
):
    row_count, model_width = stream_rows.shape
    dp_count = lax.axis_size("dp")
    expert_count = lax.axis_size("expert")
    seq_len = row_count * dp_count
    my_block = lax.axis_index("dp")
    both = ("dp", "expert")
    cores, ys = 2, 4
    grid = (cores, ys, expert_count // (cores * ys))
    own_in = gate_up[0].T
    own_out = down_weight[0]
    sent = own_in.shape[0] // 32 * 16
    near_in = lax.ppermute(own_in[:sent], "dp", [(d, d + 1 - 2 * (d % 2)) for d in range(dp_count)])

    share = row_count // expert_count
    row_id = jnp.arange(row_count, dtype=jnp.int32)
    pack = destination // seq_len
    rank = jnp.sum(
        ((pack[:, None] == pack[None, :]) & (row_id[None, :] < row_id[:, None])).astype(jnp.int32), axis=1
    )
    send_slot = pack * share + rank
    sender = (row_id[:, None] == send_slot[None, :]).astype(bf16)
    place = jnp.broadcast_to((destination % row_count).astype(bf16)[:, None], (row_count, 128))
    attention_rows = jnp.concatenate([query_rows, key_value_rows, place], axis=1)
    query_width = query_rows.shape[1]
    memory_width = key_value_rows.shape[1]

    def exchange(rows):
        width = rows.shape[1]
        moved = lax.all_to_all(
            pick(sender, rows).reshape(expert_count, share, width),
            "expert",
            split_axis=0,
            concat_axis=0,
            tiled=True,
        )
        return moved.reshape(row_count, width)

    got = exchange(attention_rows)
    got_stream = exchange(stream_rows)
    place_got = got[:, query_width + memory_width].astype(jnp.int32)
    settle = (row_id[:, None] == place_got[None, :]).astype(bf16)
    memory = pick(settle, got[:, query_width : query_width + memory_width])
    queries = pick(settle, got[:, :query_width])
    stream = jnp.dot(settle, got_stream, preferred_element_type=f32)

    group_size = HEADS // KV_HEADS
    key_width = KV_HEADS * HEAD_DIM
    seg_ends = jnp.cumsum(lengths[0])[:-1]
    query_position = my_block * row_count + row_id
    query_segment = segment_number(seg_ends, query_position)
    query_heads = queries.reshape(row_count, KV_HEADS, group_size, HEAD_DIM)

    def shift(value, step):
        if step == 0:
            return value
        return lax.ppermute(value, "dp", [(x, (x + step) % dp_count) for x in range(dp_count)])

    section = jnp.concatenate([shift(memory, s) for s in range(dp_count)], axis=0)
    key_position = jnp.concatenate(
        [lax.rem(my_block - s + dp_count, dp_count) * row_count + row_id for s in range(dp_count)]
    )
    key_count = section.shape[0]
    key_segment = segment_number(seg_ends, key_position)
    visible = (query_segment[:, None] == key_segment[None, :]) & (
        key_position[None, :] <= query_position[:, None]
    )
    key_block = section[:, :key_width].reshape(key_count, KV_HEADS, HEAD_DIM)
    value_block = section[:, key_width:].reshape(key_count, KV_HEADS, HEAD_DIM)
    scores = jnp.einsum(
        "tkgd,nkd->kgtn", query_heads, key_block, preferred_element_type=f32
    ) * HEAD_DIM ** (-0.5)
    scores = jnp.where(visible, scores, masked_score)
    row_max = jnp.max(scores, axis=-1)
    weights = jnp.where(visible, jnp.exp(scores - row_max[..., None]), 0.0)
    denominator = jnp.sum(weights, axis=-1)
    numerator = jnp.einsum(
        "kgtn,nkd->kgtd", weights.astype(bf16), value_block, preferred_element_type=f32
    )
    context = (
        (numerator / denominator[..., None])
        .transpose(2, 0, 1, 3)
        .reshape(row_count, HEADS * HEAD_DIM)
        .astype(bf16)
    )
    parts = []
    for s in range(dp_count):
        part = jnp.dot(shift(context, s), out_weight, preferred_element_type=f32).astype(bf16)
        parts.append(shift(part, (dp_count - s) % dp_count))
    order = lax.rem(jnp.arange(dp_count, dtype=jnp.int32) - my_block + dp_count, dp_count)
    update = jnp.stack(parts)[order].transpose(1, 0, 2).reshape(row_count, model_width)
    residual = stream + update.astype(f32)
    normed = (
        residual * lax.rsqrt(jnp.mean(residual * residual, axis=-1, keepdims=True) + norm_eps)
    ).astype(bf16)

    entry_count = row_count * TOPK
    capacity = entry_count // expert_count
    flat_index = expert_index.reshape(entry_count)
    onehot = (flat_index[:, None] == jnp.arange(expert_count, dtype=jnp.int32)[None, :]).astype(
        jnp.int32
    )
    slot_index = jnp.sum(onehot * (jnp.cumsum(onehot, axis=0) - 1), axis=1)
    kept_mask = slot_index < capacity
    slots = expert_count * capacity
    slab = jnp.arange(expert_count, dtype=jnp.int32)
    holder = peer(lax.axis_index("expert"), slab, 1, *grid)
    slab_expert = jnp.repeat(holder, capacity)
    slab_slot = jnp.tile(jnp.arange(capacity, dtype=jnp.int32), expert_count)
    slot_id = slab_expert * capacity + slab_slot
    target = jnp.where(kept_mask, flat_index * capacity + slot_index, slots).reshape(row_count, TOPK)
    dispatch = jnp.zeros((slots, row_count), f32)
    combine = jnp.zeros((row_count, slots), f32)
    entry_weight = router_weights.reshape(row_count, TOPK)
    for k in range(TOPK):
        dispatch = dispatch + (slot_id[:, None] == target[None, :, k]).astype(f32)
        combine = combine + jnp.where(target[:, k, None] == slot_id[None, :], entry_weight[:, k, None], 0.0)
    high = lax.reduce_precision(combine, 8, 7)
    low = (combine - high).astype(bf16)
    combine = jnp.stack([high.astype(bf16), low])
    scored = experts(grid, sent, dispatch.astype(bf16), normed, residual, combine, own_in, near_in, own_out)
    return scored.reshape(1, row_count, model_width)


def solution(mesh):
    placed = (
        P(("dp", "expert"), None),
        P(("dp", "expert"), None),
        P(("dp", "expert"), None),
        P(("dp", "expert")),
        P("expert", None),
        P(None, "dp"),
        P("expert", "dp", None),
        P("expert", "dp", None),
        P("expert", None, "dp"),
        P("expert", "dp", None),
    )
    return jax.shard_map(
        on_device, mesh=mesh, in_specs=placed, out_specs=P("expert", "dp", None), check_vma=False
    )
```

profile of v0, /device:TPU:1, one launch (start us, length us, event | category | flops | bytes accessed | tf_op | source)
XLA Modules:
  0.0 378.1 jit_solution(3549512695195075164)
XLA Ops:
  1.1 2.3 convolution_convert_fusion.1
  3.4 2.7 reshape.821
  6.1 13.5 %all-to-all-start = ((bf16[64,2,2688]{2,1,0:T(2,128)(2,1)}), bf16[64,2,2688]{2,1,0:T(2,128)(2,1)}, u32[]{:S(2)}, u32[]{:S(2)}) async-start(bf16[64,2,2688]{2,1,0:T(2,128)(2,1)} %reshape.821), calls=%async_computation | async-start | bytes 1376256 | tf_op jit(solution)/shard_map/all_to_all | solution.py:354
  19.6 3.1 slice.85
  24.4 2.3 convolution_convert_fusion
  26.7 2.3 copy.59
  29.0 2.8 reshape.823
  35.6 4.9 %all-to-all-done = bf16[64,2,2688]{2,1,0:T(2,128)(2,1)} async-done(((bf16[64,2,2688]{2,1,0:T(2,128)(2,1)}), bf16[64,2,2688]{2,1,0:T(2,128)(2,1)}, u32[]{:S(2)}, u32[]{:S(2)}) %all-to-all-start) | async-done | bytes 688160 | tf_op jit(solution)/shard_map/all_to_all | solution.py:354
  40.5 6.1 %all-to-all-start.1 = ((bf16[64,2,2880]{2,1,0:T(2,128)(2,1)}), bf16[64,2,2880]{2,1,0:T(2,128)(2,1)}, u32[]{:S(2)}, u32[]{:S(2)}) async-start(bf16[64,2,2880]{2,1,0:T(2,128)(2,1)} %reshape.823), calls=%async_computation.1 | async-start | bytes 1507328 | tf_op jit(solution)/shard_map/all_to_all | solution.py:354
  46.6 2.8 reshape.822
  53.2 2.5 collective-permute-start.1
  59.1 11.8 %collective-permute-done = bf16[128,512]{1,0:T(8,128)(2,1)} collective-permute-done((bf16[128,512]{1,0:T(8,128)(2,1)}, bf16[128,512]{1,0:T(8,128)(2,1)}, u32[]{:S(2)}, u32[]{:S(2)}) %collective-permute-start) | collective-permute-done | bytes 131104 | tf_op jit(solution)/shard_map/ppermute | solution.py:381
  70.9 6.0 %collective-permute-done.1 = bf16[128,512]{1,0:T(8,128)(2,1)} collective-permute-done((bf16[128,512]{1,0:T(8,128)(2,1)}, bf16[128,512]{1,0:T(8,128)(2,1)}, u32[]{:S(2)}, u32[]{:S(2)}) %collective-permute-start.1) | collective-permute-done | bytes 131104 | tf_op jit(solution)/shard_map/ppermute | solution.py:381
  79.1 6.6 %fusion.59 = (f32[4,8,128]{2,1,0:T(8,128)S(1)}, bf16[4,8,128,512]{2,3,1,0:T(8,128)(2,1)}) fusion(pred[128,512]{0,1:T(8,128)(4,1)S(1)} %compare_and_fusion, bf16[512,4,64,1]{0,2,3,1:T(8,128)(2,1)} %bitcast.97, bf16[128,4,8,64]{0,3,2,1:T(8,128)(2,1)} %bitcast.96), kind=kOutput, calls=%fused_computation.137 | convolution fusion | flops 281018880 | bytes 5062656 | tf_op jit(solution)/shard_map/sub | solution.py:399
  85.7 3.8 %fusion.13 = bf16[128,4,8,64]{0,3,2,1:T(8,128)(2,1)} fusion(bf16[512,4,64,1]{0,2,3,1:T(8,128)(2,1)S(1)} %bitcast.98, bf16[4,8,128,512]{2,3,1,0:T(8,128)(2,1)} %get-tuple-element.20, f32[128,4,8]{0,2,1:T(8,128)S(1)} %bitcast.105), kind=kOutput, calls=%fused_computation.18 | convolution fusion | flops 268959744 | bytes 4997120 | tf_op jit(solution)/shard_map/kgtn,nkd->kgtd/dot_general | solution.py:401
  91.9 2.9 reshape.824
  96.9 17.3 %collective-permute-done.3 = bf16[128,2048]{0,1:T(8,128)(2,1)S(1)} collective-permute-done((bf16[128,2048]{0,1:T(8,128)(2,1)}, bf16[128,2048]{0,1:T(8,128)(2,1)S(1)}, u32[]{:S(2)}, u32[]{:S(2)}) %collective-permute-start.3) | collective-permute-done | bytes 524320 | tf_op jit(solution)/shard_map/ppermute | solution.py:381
  123.2 4.7 %collective-permute-done.8 = bf16[128,720]{0,1:T(8,128)(2,1)S(1)} collective-permute-done((bf16[128,720]{0,1:T(8,128)(2,1)S(1)}, bf16[128,720]{0,1:T(8,128)(2,1)S(1)}, u32[]{:S(2)}, u32[]{:S(2)}) %collective-permute-start.8) | collective-permute-done | bytes 184352 | tf_op jit(solution)/shard_map/ppermute | solution.py:381
  128.9 2.6 gather_fusion
  132.7 2.8 multiply_reduce_fusion
  135.5 3.0 copy.64.residual
  138.5 2.4 multiply_convert_fusion.normed
  140.9 234.9 %experts.1 = bf16[128,2880]{1,0:T(8,128)(2,1)} custom-call(bf16[512,128]{1,0:T(8,128)(2,1)} %add_convert_fusion.dispatch, bf16[128,2880]{1,0:T(8,128)(2,1)} %multiply_convert_fusion.normed, f32[128,2880]{1,0:T(8,128)} %copy.64.residual, bf16[2,128,512]{2,1,0:T(8,128)(2,1)} %pad_maximum_fusion.2.combine, bf16[720,2880]{1,0:T(8,128)(2,1)} %bitcast.94, ...), custom_call_target="tpu_custom_call" | custom-call | flops 15032385536 | bytes 31457280 | tf_op jit(solution)/shard_map/experts/pallas_call | solution.py:285
  375.9 2.3 copy.66
  (87 shorter events, 31.5 us)
Async XLA Ops:
  0.0 114.2 %copy-start = (bf16[2048,720]{0,1:T(8,128)(2,1)S(1)}, bf16[2048,720]{0,1:T(8,128)(2,1)}, u32[]{:S(2)}) copy-start(bf16[2048,720]{0,1:T(8,128)(2,1)} %param.15) | copy-start | bytes 8847364
  6.1 17.7 %copy-start.8 = (s32[1,128,4]{1,2,0:T(4,128)S(1)}, s32[1,128,4]{1,2,0:T(4,128)}, u32[]{:S(2)}) copy-start(s32[1,128,4]{1,2,0:T(4,128)} %param.16) | copy-start | bytes 6148
  6.1 18.1 %copy-start.10 = (s32[1,3]{1,0:T(1,128)S(1)}, s32[1,3]{1,0:T(1,128)}, u32[]{:S(2)}) copy-start(s32[1,3]{1,0:T(1,128)} %param.14) | copy-start | bytes 40
  6.1 34.4 %all-to-all-start = ((bf16[64,2,2688]{2,1,0:T(2,128)(2,1)}), bf16[64,2,2688]{2,1,0:T(2,128)(2,1)}, u32[]{:S(2)}, u32[]{:S(2)}) async-start(bf16[64,2,2688]{2,1,0:T(2,128)(2,1)} %reshape.821), calls=%async_computation | async-start | bytes 1376256 | tf_op jit(solution)/shard_map/all_to_all | solution.py:354
  22.6 118.3 %collective-permute-start.9 = (bf16[352,2880]{1,0:T(8,128)(2,1)}, bf16[352,2880]{1,0:T(8,128)(2,1)}, u32[]{:S(2)}, u32[]{:S(2)}) collective-permute-start(bf16[352,2880]{1,0:T(8,128)(2,1)} %slice.85), channel_id=1, source_target_pairs={{0,64},{64,0},{128,192},{192,128},{1,65},{65,1},{129,193},{193,129... | collective-permute-start | bytes 6082568 | tf_op jit(solution)/shard_map/ppermute | solution.py:337
  24.1 10.7 %copy-start.9 = (f32[1,128,4]{1,2,0:T(4,128)S(1)}, f32[1,128,4]{1,2,0:T(4,128)}, u32[]{:S(2)}) copy-start(f32[1,128,4]{1,2,0:T(4,128)} %param.17) | copy-start | bytes 6148
  40.5 51.4 %all-to-all-start.1 = ((bf16[64,2,2880]{2,1,0:T(2,128)(2,1)}), bf16[64,2,2880]{2,1,0:T(2,128)(2,1)}, u32[]{:S(2)}, u32[]{:S(2)}) async-start(bf16[64,2,2880]{2,1,0:T(2,128)(2,1)} %reshape.823), calls=%async_computation.1 | async-start | bytes 1507328 | tf_op jit(solution)/shard_map/all_to_all | solution.py:354
  52.0 18.9 %collective-permute-start = (bf16[128,512]{1,0:T(8,128)(2,1)}, bf16[128,512]{1,0:T(8,128)(2,1)}, u32[]{:S(2)}, u32[]{:S(2)}) collective-permute-start(bf16[128,512]{1,0:T(8,128)(2,1)} %convolution_convert_fusion.7), channel_id=1, source_target_pairs={{0,64},{64,128},{128,192},{192,0},{1,65},{65,129},{129,193},{193,1... | collective-permute-start | bytes 393224 | tf_op jit(solution)/shard_map/ppermute | solution.py:381
  53.2 23.7 %collective-permute-start.1 = (bf16[128,512]{1,0:T(8,128)(2,1)}, bf16[128,512]{1,0:T(8,128)(2,1)}, u32[]{:S(2)}, u32[]{:S(2)}) collective-permute-start(bf16[128,512]{1,0:T(8,128)(2,1)} %convolution_convert_fusion.7), channel_id=1, source_target_pairs={{0,128},{64,192},{128,0},{192,64},{1,129},{65,193},{129,1},{193,65... | collective-permute-start | bytes 393224 | tf_op jit(solution)/shard_map/ppermute | solution.py:381
  55.6 21.3 %collective-permute-start.2 = (bf16[128,512]{1,0:T(8,128)(2,1)}, bf16[128,512]{1,0:T(8,128)(2,1)}, u32[]{:S(2)}, u32[]{:S(2)}) collective-permute-start(bf16[128,512]{1,0:T(8,128)(2,1)} %convolution_convert_fusion.7), channel_id=1, source_target_pairs={{0,192},{64,0},{128,64},{192,128},{1,193},{65,1},{129,65},{193,129... | collective-permute-start | bytes 393224 | tf_op jit(solution)/shard_map/ppermute | solution.py:381
  85.7 3.9 %copy-start.1 = (s32[128]{0:T(128)S(1)}, s32[128]{0:T(128)}, u32[]{:S(2)}) copy-start(s32[128]{0:T(128)} %get-tuple-element.6) | copy-start | bytes 1540
  85.7 3.9 %copy-start.2 = (s32[128]{0:T(128)S(1)}, s32[128]{0:T(128)}, u32[]{:S(2)}) copy-start(s32[128]{0:T(128)} %get-tuple-element.7) | copy-start | bytes 1540
  85.7 3.9 %copy-start.3 = (s32[128]{0:T(128)S(1)}, s32[128]{0:T(128)}, u32[]{:S(2)}) copy-start(s32[128]{0:T(128)} %get-tuple-element.8) | copy-start | bytes 1540
  85.7 3.9 %copy-start.4 = (f32[128]{0:T(128)S(1)}, f32[128]{0:T(128)}, u32[]{:S(2)}) copy-start(f32[128]{0:T(128)} %get-tuple-element.13) | copy-start | bytes 1540
  85.7 3.9 %copy-start.5 = (f32[128]{0:T(128)S(1)}, f32[128]{0:T(128)}, u32[]{:S(2)}) copy-start(f32[128]{0:T(128)} %get-tuple-element.14) | copy-start | bytes 1540
  85.7 3.9 %copy-start.6 = (f32[128]{0:T(128)S(1)}, f32[128]{0:T(128)}, u32[]{:S(2)}) copy-start(f32[128]{0:T(128)} %get-tuple-element.15) | copy-start | bytes 1540
  85.7 3.9 %copy-start.7 = (f32[128]{0:T(128)S(1)}, f32[128]{0:T(128)}, u32[]{:S(2)}) copy-start(f32[128]{0:T(128)} %get-tuple-element.16) | copy-start | bytes 1540
  89.5 24.7 %collective-permute-start.3 = (bf16[128,2048]{0,1:T(8,128)(2,1)}, bf16[128,2048]{0,1:T(8,128)(2,1)S(1)}, u32[]{:S(2)}, u32[]{:S(2)}) collective-permute-start(bf16[128,2048]{0,1:T(8,128)(2,1)} %bitcast.14), channel_id=1, source_target_pairs={{0,64},{64,128},{128,192},{192,0},{1,65},{65,129},{129,193},{193,1... | collective-permute-start | bytes 1572872 | tf_op jit(solution)/shard_map/ppermute | solution.py:381
  90.5 24.7 %collective-permute-start.5 = (bf16[128,2048]{0,1:T(8,128)(2,1)}, bf16[128,2048]{0,1:T(8,128)(2,1)}, u32[]{:S(2)}, u32[]{:S(2)}) collective-permute-start(bf16[128,2048]{0,1:T(8,128)(2,1)} %bitcast.14), channel_id=1, source_target_pairs={{0,128},{64,192},{128,0},{192,64},{1,129},{65,193},{129,1},{193,65... | collective-permute-start | bytes 1572872 | tf_op jit(solution)/shard_map/ppermute | solution.py:381
  94.8 22.5 %collective-permute-start.7 = (bf16[128,2048]{0,1:T(8,128)(2,1)}, bf16[128,2048]{0,1:T(8,128)(2,1)S(1)}, u32[]{:S(2)}, u32[]{:S(2)}) collective-permute-start(bf16[128,2048]{0,1:T(8,128)(2,1)} %bitcast.14), channel_id=1, source_target_pairs={{0,192},{64,0},{128,64},{192,128},{1,193},{65,1},{129,65},{193,129... | collective-permute-start | bytes 1572872 | tf_op jit(solution)/shard_map/ppermute | solution.py:381
  115.1 6.8 %collective-permute-start.4 = (bf16[128,720]{0,1:T(8,128)(2,1)S(1)}, bf16[128,720]{0,1:T(8,128)(2,1)S(1)}, u32[]{:S(2)}, u32[]{:S(2)}) collective-permute-start(bf16[128,720]{0,1:T(8,128)(2,1)S(1)} %convolution_convert_fusion.5), channel_id=1, source_target_pairs={{0,192},{64,0},{128,64},{192,128},{1,193},{65,1},{129,65},{193,129... | collective-permute-start | bytes 552968 | tf_op jit(solution)/shard_map/ppermute | solution.py:381
  117.2 6.0 %collective-permute-start.6 = (bf16[128,720]{0,1:T(8,128)(2,1)S(1)}, bf16[128,720]{0,1:T(8,128)(2,1)S(1)}, u32[]{:S(2)}, u32[]{:S(2)}) collective-permute-start(bf16[128,720]{0,1:T(8,128)(2,1)S(1)} %convolution_convert_fusion.4), channel_id=1, source_target_pairs={{0,128},{64,192},{128,0},{192,64},{1,129},{65,193},{129,1},{193,65... | collective-permute-start | bytes 552968 | tf_op jit(solution)/shard_map/ppermute | solution.py:381
  118.3 9.6 %collective-permute-start.8 = (bf16[128,720]{0,1:T(8,128)(2,1)S(1)}, bf16[128,720]{0,1:T(8,128)(2,1)S(1)}, u32[]{:S(2)}, u32[]{:S(2)}) collective-permute-start(bf16[128,720]{0,1:T(8,128)(2,1)S(1)} %convolution_convert_fusion.3), channel_id=1, source_target_pairs={{0,64},{64,128},{128,192},{192,0},{1,65},{65,129},{129,193},{193,1... | collective-permute-start | bytes 552968 | tf_op jit(solution)/shard_map/ppermute | solution.py:381
where the time goes:
time: 380 us; the launch traced here: 378 us
  Pallas kernels  235 us (62%)
  waiting for transfers between devices  45.9 us (12%)
  starting transfers between devices  30.1 us (8%)
  local copies, waits for them, and re-layouts  28.7 us (8%)
  matrix products  26.7 us (7%)
  other arithmetic  11.4 us (3%)
    pallas_call x1, Pallas kernels, experts(): pl.pallas_call(functools.partial(expert_kernel, grid, sent), out_shape=ja...  235 us
    ppermute x9, waiting for transfers between devices, shift(): lax.ppermute(value, 'dp', [(x, (x + step) % dp_count) for x in range(dp_c...  41 us
    all_to_all x2, starting transfers between devices, exchange(): lax.all_to_all(pick(sender, rows).reshape(expert_count, share, width), 'e...  19.5 us
    ppermute x9, starting transfers between devices, shift(): lax.ppermute(value, 'dp', [(x, (x + step) % dp_count) for x in range(dp_c...  9.41 us
    dot_general x4, matrix products, pick(): return jnp.dot(matrix, rows, preferred_element_type=f32).astype(bf16)  7.7 us
  transfers between devices with their start and end apart: 12, of which 6 were waited for; matrix products, arithmetic and copies ran while one was open for 15% of the time, Pallas kernels for 0%

commit v1 on v0

--- a/solution.py
+++ b/solution.py
@@ -29,8 +29,10 @@
 
 def relation(index, cores, ys, zs):
     per = zs * cores
+    half = max(zs // 2, 1)
     chunk, rest = index // per, index % per
-    dz = rest // cores
+    turn = rest // cores
+    dz = (turn % 2) * (half + turn // 2) + (1 - turn % 2) * ((half - turn // 2) % half)
     return dz, (chunk + zs * ys - dz) % ys, rest % cores
 
 
@@ -43,9 +45,12 @@
     return (z * ys + y) * cores + c
 
 
+def weight_pair(x, core):
+    return (x + 5 - 2 * ((x + core) % 2)) % 4
+
+
 def expert_kernel(
     grid,
-    sent,
     dispatch,
     normed,
     residual,
@@ -81,42 +86,49 @@
     cores, ys, zs = grid
     x = lax.axis_index("dp")
     e = lax.axis_index("expert")
-    odd = x % 2
-    pair = (x + 1 - 2 * odd, e)
-    twin = ((x + 2 * odd + 3) % 4, e)
+    pair = (weight_pair(x, e % cores), e)
+    twin = (weight_pair(x, 1 - e % cores), e)
     slabs, capacity, width = out_buf.shape
     per = slabs // 4
     rows = per * capacity
     columns = raw_in.shape[1]
     units = columns // 2
     padded = split_in.shape[1] // 2
-    rest = columns - sent
+    count = cores * ys * zs
+
+    barrier = pltpu.get_barrier_semaphore()
+
+    def greet(step, carry):
+        pl.semaphore_signal(
+            barrier, inc=1, device_id=(x, (e + step) % count), device_id_type=pl.DeviceIdType.MESH
+        )
+        return carry
+
+    lax.fori_loop(1, count, greet, 0)
+    pl.semaphore_signal(barrier, inc=1, device_id=pair, device_id_type=pl.DeviceIdType.MESH)
+    pl.semaphore_signal(barrier, inc=1, device_id=twin, device_id_type=pl.DeviceIdType.MESH)
 
     def remote(src, dst, ssem, rsem, device):
         return pltpu.make_async_remote_copy(
             src_ref=src, dst_ref=dst, send_sem=ssem, recv_sem=rsem, device_id=device, device_id_type=pl.DeviceIdType.MESH
         )
 
-    weight_in = remote(
-        own_in.at[pl.ds(sent, rest)], raw_in.at[1, pl.ds(sent, rest)], weight_send.at[0], weight_recv.at[0], pair
-    )
-    weight_out = remote(own_out, raw_out.at[1], weight_send.at[1], weight_recv.at[1], pair)
-    weight_in.start()
-    weight_out.start()
     load_own = pltpu.make_async_copy(own_in, raw_in.at[0], local_sem.at[0])
-    load_near = pltpu.make_async_copy(near_in, raw_in.at[1, pl.ds(0, sent)], local_sem.at[1])
+    load_near = pltpu.make_async_copy(near_in, raw_in.at[1], local_sem.at[1])
     load_out = pltpu.make_async_copy(own_out, raw_out.at[0], local_sem.at[2])
     load_own.start()
     load_near.start()
     load_out.start()
+    weight_out = remote(own_out, raw_out.at[1], weight_send, weight_recv, pair)
 
     def chunk_of(ref, c):
         return ref.at[pl.ds(c * per, per)]
 
-    def send_dispatch(c, carry):
+    def pack_dispatch(c):
         picked = jnp.dot(dispatch[pl.ds(c * rows, rows), :], normed[...], preferred_element_type=f32)
         out_buf[pl.ds(c * per, per)] = picked.astype(bf16).reshape(per, capacity, width)
 
+    def send_dispatch(c):
         def one(m, carry):
             index = c * per + m
             remote(
@@ -125,9 +137,17 @@
             return carry
 
         lax.fori_loop(jnp.where(c == 0, 1, 0), per, one, 0)
+
+    def begin(c, carry):
+        pack_dispatch(c)
+        send_dispatch(c)
         return carry
 
-    lax.fori_loop(0, 4, send_dispatch, 0)
+    pack_dispatch(0)
+    pl.semaphore_wait(barrier, count + 1)
+    send_dispatch(0)
+    weight_out.start()
+    lax.fori_loop(1, 4, begin, 0)
     in_own[0] = out_buf[0]
 
     row = lax.broadcasted_iota(jnp.int32, (2 * padded, columns), 0)
@@ -143,9 +163,9 @@
 
     load_own.wait()
     separate(0)
-
-    def lead(ref, c):
-        return ref.at[pl.ds(c * per, per)]
+    load_near.wait()
+    separate(1)
+    load_out.wait()
 
     def wait_own(c):
         @pl.when(c == 0)
@@ -220,10 +240,6 @@
 
         @pl.when(t == 1)
         def _():
-            load_near.wait()
-            load_out.wait()
-            weight_in.wait()
-            separate(1)
             weight_out.wait()
 
         @pl.when((t >= 1) & (t < 5))
@@ -269,7 +285,7 @@
         result[:, cols] = (residual[:, cols] + mixed).astype(bf16)
 
 
-def experts(grid, sent, dispatch, normed, residual, combine, own_in, near_in, own_out):
+def experts(grid, dispatch, normed, residual, combine, own_in, near_in, own_out):
     slots, row_count = dispatch.shape
     width = normed.shape[1]
     columns = own_in.shape[0]
@@ -283,7 +299,7 @@
     dma = pltpu.SemaphoreType.DMA
     buffer = pltpu.VMEM((slabs, capacity, width), bf16)
     return pl.pallas_call(
-        functools.partial(expert_kernel, grid, sent),
+        functools.partial(expert_kernel, grid),
         out_shape=jax.ShapeDtypeStruct((row_count, width), bf16),
         in_specs=[vmem, vmem, vmem, vmem, hbm, hbm, hbm],
         out_specs=vmem,
@@ -301,11 +317,11 @@
             buffer,
             buffer,
             dma((3,)),
-            dma((2,)),
-            dma((2,)),
+            dma,
+            dma,
         ]
         + [dma((4,))] * 8,
-        compiler_params=pltpu.CompilerParams(has_side_effects=True, vmem_limit_bytes=60 << 20),
+        compiler_params=pltpu.CompilerParams(collective_id=1, has_side_effects=True, vmem_limit_bytes=60 << 20),
         cost_estimate=pl.CostEstimate(flops=14 << 30, bytes_accessed=30 << 20, transcendentals=0),
         name="experts",
     )(dispatch, normed, residual, combine, own_in, near_in, own_out)
@@ -333,8 +349,12 @@
     grid = (cores, ys, expert_count // (cores * ys))
     own_in = gate_up[0].T
     own_out = down_weight[0]
-    sent = own_in.shape[0] // 32 * 16
-    near_in = lax.ppermute(own_in[:sent], "dp", [(d, d + 1 - 2 * (d % 2)) for d in range(dp_count)])
+    swap = [
+        (d * expert_count + e, weight_pair(d, e % cores) * expert_count + e)
+        for d in range(dp_count)
+        for e in range(expert_count)
+    ]
+    near_in = lax.ppermute(own_in, ("dp", "expert"), swap)
 
     share = row_count // expert_count
     row_id = jnp.arange(row_count, dtype=jnp.int32)
@@ -442,7 +462,7 @@
     high = lax.reduce_precision(combine, 8, 7)
     low = (combine - high).astype(bf16)
     combine = jnp.stack([high.astype(bf16), low])
-    scored = experts(grid, sent, dispatch.astype(bf16), normed, residual, combine, own_in, near_in, own_out)
+    scored = experts(grid, dispatch.astype(bf16), normed, residual, combine, own_in, near_in, own_out)
     return scored.reshape(1, row_count, model_width)
 
 

time: 380 us -> 288 us (0.76)
  Pallas kernels: 235 us -> 145 us
  starting transfers between devices: 30.1 us -> 34.1 us
    pallas_call x1, Pallas kernels: 235 us -> 145 us  [experts(): pl.pallas_call(functools.partial(expert_kernel, grid), out_shape=jax.Shap...]
    ppermute x9, waiting for transfers between devices: 41 us -> 37.1 us  [shift(): lax.ppermute(value, 'dp', [(x, (x + step) % dp_count) for x in range(dp_c...]
  transfers between devices with their start and end apart: 12 -> 12, of which waited for: 6 -> 5; matrix products, arithmetic and copies ran while one was open for 15% -> 19% of each run, Pallas kernels for 0% -> 0%
where the time goes in v1:
time: 288 us; the launch traced here: 287 us
  Pallas kernels  145 us (50%)
  waiting for transfers between devices  43.7 us (15%)
  starting transfers between devices  34.1 us (12%)
  matrix products  26.8 us (9%)
  local copies, waits for them, and re-layouts  25.6 us (9%)
  other arithmetic  11.4 us (4%)
    pallas_call x1, Pallas kernels, experts(): pl.pallas_call(functools.partial(expert_kernel, grid), out_shape=jax.Shap...  145 us
    ppermute x9, waiting for transfers between devices, shift(): lax.ppermute(value, 'dp', [(x, (x + step) % dp_count) for x in range(dp_c...  37.1 us
    all_to_all x2, starting transfers between devices, exchange(): lax.all_to_all(pick(sender, rows).reshape(expert_count, share, width), 'e...  19.4 us
    ppermute x9, starting transfers between devices, shift(): lax.ppermute(value, 'dp', [(x, (x + step) % dp_count) for x in range(dp_c...  12.1 us
    dot_general x4, matrix products, pick(): return jnp.dot(matrix, rows, preferred_element_type=f32).astype(bf16)  7.7 us
    sub x1, matrix products, on_device(): weights = jnp.where(visible, jnp.exp(scores - row_max[..., None]), 0.0)  6.64 us
    all_to_all x2, waiting for transfers between devices, exchange(): lax.all_to_all(pick(sender, rows).reshape(expert_count, share, width), 'e...  6.62 us
    dot_general x4, matrix products, on_device(): jnp.dot(shift(context, s), out_weight, preferred_element_type=f32)  5.8 us
  transfers between devices with their start and end apart: 12, of which 5 were waited for; matrix products, arithmetic and copies ran while one was open for 19% of the time, Pallas kernels for 0%

profile of v1, /device:TPU:1, one launch (start us, length us, event | category | flops | bytes accessed | tf_op | source)
XLA Modules:
  0.0 287.4 jit_solution(8609923388579295757)
XLA Ops:
  1.1 2.3 convolution_convert_fusion.1
  3.4 2.7 reshape.821
  6.1 13.3 %all-to-all-start = ((bf16[64,2,2688]{2,1,0:T(2,128)(2,1)}), bf16[64,2,2688]{2,1,0:T(2,128)(2,1)}, u32[]{:S(2)}, u32[]{:S(2)}) async-start(bf16[64,2,2688]{2,1,0:T(2,128)(2,1)} %reshape.821), calls=%async_computation | async-start | bytes 1376256 | tf_op jit(solution)/shard_map/all_to_all | solution.py:374
  19.4 2.6 collective-permute-start.9
  24.5 2.3 convolution_convert_fusion
  26.9 2.3 copy.59
  29.1 2.8 reshape.823
  33.7 6.6 %all-to-all-done = bf16[64,2,2688]{2,1,0:T(2,128)(2,1)} async-done(((bf16[64,2,2688]{2,1,0:T(2,128)(2,1)}), bf16[64,2,2688]{2,1,0:T(2,128)(2,1)}, u32[]{:S(2)}, u32[]{:S(2)}) %all-to-all-start) | async-done | bytes 688160 | tf_op jit(solution)/shard_map/all_to_all | solution.py:374
  40.4 6.1 %all-to-all-start.1 = ((bf16[64,2,2880]{2,1,0:T(2,128)(2,1)}), bf16[64,2,2880]{2,1,0:T(2,128)(2,1)}, u32[]{:S(2)}, u32[]{:S(2)}) async-start(bf16[64,2,2880]{2,1,0:T(2,128)(2,1)} %reshape.823), calls=%async_computation.1 | async-start | bytes 1507328 | tf_op jit(solution)/shard_map/all_to_all | solution.py:374
  46.4 2.8 reshape.822
  51.8 2.5 collective-permute-start.2
  57.8 16.1 %collective-permute-done.2 = bf16[128,512]{1,0:T(8,128)(2,1)} collective-permute-done((bf16[128,512]{1,0:T(8,128)(2,1)}, bf16[128,512]{1,0:T(8,128)(2,1)}, u32[]{:S(2)}, u32[]{:S(2)}) %collective-permute-start.2) | collective-permute-done | bytes 131104 | tf_op jit(solution)/shard_map/ppermute | solution.py:401
  76.1 6.6 %fusion.62 = (f32[4,8,128]{2,1,0:T(8,128)S(1)}, bf16[4,8,128,512]{2,3,1,0:T(8,128)(2,1)}) fusion(pred[128,512]{0,1:T(8,128)(4,1)S(1)} %compare_and_fusion, bf16[512,4,64,1]{0,2,3,1:T(8,128)(2,1)} %bitcast.95, bf16[128,4,8,64]{0,3,2,1:T(8,128)(2,1)} %bitcast.94), kind=kOutput, calls=%fused_computation.148 | convolution fusion | flops 281018880 | bytes 5062656 | tf_op jit(solution)/shard_map/sub | solution.py:419
  82.7 3.8 %fusion.13 = bf16[128,4,8,64]{0,3,2,1:T(8,128)(2,1)} fusion(bf16[512,4,64,1]{0,2,3,1:T(8,128)(2,1)S(1)} %bitcast.96, bf16[4,8,128,512]{2,3,1,0:T(8,128)(2,1)} %get-tuple-element.20, f32[128,4,8]{0,2,1:T(8,128)S(1)} %bitcast.105), kind=kOutput, calls=%fused_computation.18 | convolution fusion | flops 268959744 | bytes 4997120 | tf_op jit(solution)/shard_map/kgtn,nkd->kgtd/dot_general | solution.py:421
  86.6 3.1 %collective-permute-start.7 = (bf16[128,2048]{0,1:T(8,128)(2,1)}, bf16[128,2048]{0,1:T(8,128)(2,1)S(1)}, u32[]{:S(2)}, u32[]{:S(2)}) collective-permute-start(bf16[128,2048]{0,1:T(8,128)(2,1)} %bitcast.14), channel_id=1, source_target_pairs={{0,192},{64,0},{128,64},{192,128},{1,193},{65,1},{129,65},{193,129... | collective-permute-start | bytes 1572872 | tf_op jit(solution)/shard_map/ppermute | solution.py:401
  91.5 2.9 %reshape.824 = bf16[128,2880]{1,0:T(8,128)(2,1)} reshape(bf16[64,2,2880]{2,1,0:T(2,128)(2,1)} %all-to-all-done.1) | data formatting | bytes 1474560 | tf_op jit(solution)/shard_map/reshape | solution.py:381
  95.0 16.9 %collective-permute-done.7 = bf16[128,2048]{0,1:T(8,128)(2,1)S(1)} collective-permute-done((bf16[128,2048]{0,1:T(8,128)(2,1)}, bf16[128,2048]{0,1:T(8,128)(2,1)S(1)}, u32[]{:S(2)}, u32[]{:S(2)}) %collective-permute-start.7) | collective-permute-done | bytes 524320 | tf_op jit(solution)/shard_map/ppermute | solution.py:401
  114.9 4.7 %collective-permute-start.6 = (bf16[128,720]{0,1:T(8,128)(2,1)S(1)}, bf16[128,720]{0,1:T(8,128)(2,1)S(1)}, u32[]{:S(2)}, u32[]{:S(2)}) collective-permute-start(bf16[128,720]{0,1:T(8,128)(2,1)S(1)} %convolution_convert_fusion.4), channel_id=1, source_target_pairs={{0,128},{64,192},{128,0},{192,64},{1,129},{65,193},{129,1},{193,65... | collective-permute-start | bytes 552968 | tf_op jit(solution)/shard_map/ppermute | solution.py:401
  127.6 2.6 gather_fusion
  131.5 2.8 multiply_reduce_fusion
  134.3 3.0 %copy.64.residual = f32[128,2880]{1,0:T(8,128)} copy(f32[128,2880]{0,1:T(8,128)} %get-tuple-element.22) | data formatting | bytes 2949120 | tf_op jit(solution)/shard_map/add | solution.py:436
  137.3 2.4 multiply_convert_fusion.normed
  139.7 145.4 %experts.1 = bf16[128,2880]{1,0:T(8,128)(2,1)} custom-call(bf16[512,128]{1,0:T(8,128)(2,1)} %add_convert_fusion.dispatch, bf16[128,2880]{1,0:T(8,128)(2,1)} %multiply_convert_fusion.normed, f32[128,2880]{1,0:T(8,128)} %copy.64.residual, bf16[2,128,512]{2,1,0:T(8,128)(2,1)} %pad_maximum_fusion.2.combine, bf16[720,2880]{1,0:T(8,128)(2,1)} %bitcast.102, ...), custom_call_target="tpu_custom_call" | custom-call | flops 15032385536 | bytes 31457280 | tf_op jit(solution)/shard_map/experts/pallas_call | solution.py:301
  285.2 2.3 copy.66
  (86 shorter events, 28.1 us)
Async XLA Ops:
  0.0 111.9 %copy-start = (bf16[2048,720]{0,1:T(8,128)(2,1)S(1)}, bf16[2048,720]{0,1:T(8,128)(2,1)}, u32[]{:S(2)}) copy-start(bf16[2048,720]{0,1:T(8,128)(2,1)} %param.15) | copy-start | bytes 8847364
  0.0 22.0 %copy-start.8 = (s32[1,128,4]{1,2,0:T(4,128)S(1)}, s32[1,128,4]{1,2,0:T(4,128)}, u32[]{:S(2)}) copy-start(s32[1,128,4]{1,2,0:T(4,128)} %param.16) | copy-start | bytes 6148
  0.0 22.4 %copy-start.10 = (s32[1,3]{1,0:T(1,128)S(1)}, s32[1,3]{1,0:T(1,128)}, u32[]{:S(2)}) copy-start(s32[1,3]{1,0:T(1,128)} %param.14) | copy-start | bytes 40
  6.1 34.3 %all-to-all-start = ((bf16[64,2,2688]{2,1,0:T(2,128)(2,1)}), bf16[64,2,2688]{2,1,0:T(2,128)(2,1)}, u32[]{:S(2)}, u32[]{:S(2)}) async-start(bf16[64,2,2688]{2,1,0:T(2,128)(2,1)} %reshape.821), calls=%async_computation | async-start | bytes 1376256 | tf_op jit(solution)/shard_map/all_to_all | solution.py:374
  19.4 120.3 %collective-permute-start.9 = (bf16[720,2880]{1,0:T(8,128)(2,1)}, bf16[720,2880]{1,0:T(8,128)(2,1)}, u32[]{:S(2)}, u32[]{:S(2)}) collective-permute-start(bf16[720,2880]{1,0:T(8,128)(2,1)} %bitcast.101), channel_id=1, source_target_pairs={{0,64},{1,193},{2,66},{3,195},{4,68},{5,197},{6,70},{7,199},{8,72}... | collective-permute-start | bytes 12441608 | tf_op jit(solution)/shard_map/ppermute | solution.py:357
  22.2 10.7 %copy-start.9 = (f32[1,128,4]{1,2,0:T(4,128)S(1)}, f32[1,128,4]{1,2,0:T(4,128)}, u32[]{:S(2)}) copy-start(f32[1,128,4]{1,2,0:T(4,128)} %param.17) | copy-start | bytes 6148
  40.4 51.1 %all-to-all-start.1 = ((bf16[64,2,2880]{2,1,0:T(2,128)(2,1)}), bf16[64,2,2880]{2,1,0:T(2,128)(2,1)}, u32[]{:S(2)}, u32[]{:S(2)}) async-start(bf16[64,2,2880]{2,1,0:T(2,128)(2,1)} %reshape.823), calls=%async_computation.1 | async-start | bytes 1507328 | tf_op jit(solution)/shard_map/all_to_all | solution.py:374
  51.8 22.1 %collective-permute-start.2 = (bf16[128,512]{1,0:T(8,128)(2,1)}, bf16[128,512]{1,0:T(8,128)(2,1)}, u32[]{:S(2)}, u32[]{:S(2)}) collective-permute-start(bf16[128,512]{1,0:T(8,128)(2,1)} %convolution_convert_fusion.7), channel_id=1, source_target_pairs={{0,192},{64,0},{128,64},{192,128},{1,193},{65,1},{129,65},{193,129... | collective-permute-start | bytes 393224 | tf_op jit(solution)/shard_map/ppermute | solution.py:401
  54.3 19.6 %collective-permute-start.1 = (bf16[128,512]{1,0:T(8,128)(2,1)}, bf16[128,512]{1,0:T(8,128)(2,1)}, u32[]{:S(2)}, u32[]{:S(2)}) collective-permute-start(bf16[128,512]{1,0:T(8,128)(2,1)} %convolution_convert_fusion.7), channel_id=1, source_target_pairs={{0,128},{64,192},{128,0},{192,64},{1,129},{65,193},{129,1},{193,65... | collective-permute-start | bytes 393224 | tf_op jit(solution)/shard_map/ppermute | solution.py:401
  54.8 19.1 %collective-permute-start = (bf16[128,512]{1,0:T(8,128)(2,1)}, bf16[128,512]{1,0:T(8,128)(2,1)}, u32[]{:S(2)}, u32[]{:S(2)}) collective-permute-start(bf16[128,512]{1,0:T(8,128)(2,1)} %convolution_convert_fusion.7), channel_id=1, source_target_pairs={{0,64},{64,128},{128,192},{192,0},{1,65},{65,129},{129,193},{193,1... | collective-permute-start | bytes 393224 | tf_op jit(solution)/shard_map/ppermute | solution.py:401
  82.7 7.0 %copy-start.1 = (s32[128]{0:T(128)S(1)}, s32[128]{0:T(128)}, u32[]{:S(2)}) copy-start(s32[128]{0:T(128)} %get-tuple-element.6) | copy-start | bytes 1540
  82.7 7.0 %copy-start.2 = (s32[128]{0:T(128)S(1)}, s32[128]{0:T(128)}, u32[]{:S(2)}) copy-start(s32[128]{0:T(128)} %get-tuple-element.7) | copy-start | bytes 1540
  82.7 7.0 %copy-start.3 = (s32[128]{0:T(128)S(1)}, s32[128]{0:T(128)}, u32[]{:S(2)}) copy-start(s32[128]{0:T(128)} %get-tuple-element.8) | copy-start | bytes 1540
  82.7 7.0 %copy-start.4 = (f32[128]{0:T(128)S(1)}, f32[128]{0:T(128)}, u32[]{:S(2)}) copy-start(f32[128]{0:T(128)} %get-tuple-element.13) | copy-start | bytes 1540
  82.7 7.0 %copy-start.5 = (f32[128]{0:T(128)S(1)}, f32[128]{0:T(128)}, u32[]{:S(2)}) copy-start(f32[128]{0:T(128)} %get-tuple-element.14) | copy-start | bytes 1540
  82.7 7.0 %copy-start.6 = (f32[128]{0:T(128)S(1)}, f32[128]{0:T(128)}, u32[]{:S(2)}) copy-start(f32[128]{0:T(128)} %get-tuple-element.15) | copy-start | bytes 1540
  82.7 7.0 %copy-start.7 = (f32[128]{0:T(128)S(1)}, f32[128]{0:T(128)}, u32[]{:S(2)}) copy-start(f32[128]{0:T(128)} %get-tuple-element.16) | copy-start | bytes 1540
  86.6 25.3 %collective-permute-start.7 = (bf16[128,2048]{0,1:T(8,128)(2,1)}, bf16[128,2048]{0,1:T(8,128)(2,1)S(1)}, u32[]{:S(2)}, u32[]{:S(2)}) collective-permute-start(bf16[128,2048]{0,1:T(8,128)(2,1)} %bitcast.14), channel_id=1, source_target_pairs={{0,192},{64,0},{128,64},{192,128},{1,193},{65,1},{129,65},{193,129... | collective-permute-start | bytes 1572872 | tf_op jit(solution)/shard_map/ppermute | solution.py:401
  90.6 22.3 %collective-permute-start.5 = (bf16[128,2048]{0,1:T(8,128)(2,1)}, bf16[128,2048]{0,1:T(8,128)(2,1)}, u32[]{:S(2)}, u32[]{:S(2)}) collective-permute-start(bf16[128,2048]{0,1:T(8,128)(2,1)} %bitcast.14), channel_id=1, source_target_pairs={{0,128},{64,192},{128,0},{192,64},{1,129},{65,193},{129,1},{193,65... | collective-permute-start | bytes 1572872 | tf_op jit(solution)/shard_map/ppermute | solution.py:401
  94.4 25.2 %collective-permute-start.3 = (bf16[128,2048]{0,1:T(8,128)(2,1)}, bf16[128,2048]{0,1:T(8,128)(2,1)S(1)}, u32[]{:S(2)}, u32[]{:S(2)}) collective-permute-start(bf16[128,2048]{0,1:T(8,128)(2,1)} %bitcast.14), channel_id=1, source_target_pairs={{0,64},{64,128},{128,192},{192,0},{1,65},{65,129},{129,193},{193,1... | collective-permute-start | bytes 1572872 | tf_op jit(solution)/shard_map/ppermute | solution.py:401
  112.8 9.8 %collective-permute-start.8 = (bf16[128,720]{0,1:T(8,128)(2,1)S(1)}, bf16[128,720]{0,1:T(8,128)(2,1)S(1)}, u32[]{:S(2)}, u32[]{:S(2)}) collective-permute-start(bf16[128,720]{0,1:T(8,128)(2,1)S(1)} %convolution_convert_fusion.3), channel_id=1, source_target_pairs={{0,64},{64,128},{128,192},{192,0},{1,65},{65,129},{129,193},{193,1... | collective-permute-start | bytes 552968 | tf_op jit(solution)/shard_map/ppermute | solution.py:401
  114.9 9.9 %collective-permute-start.6 = (bf16[128,720]{0,1:T(8,128)(2,1)S(1)}, bf16[128,720]{0,1:T(8,128)(2,1)S(1)}, u32[]{:S(2)}, u32[]{:S(2)}) collective-permute-start(bf16[128,720]{0,1:T(8,128)(2,1)S(1)} %convolution_convert_fusion.4), channel_id=1, source_target_pairs={{0,128},{64,192},{128,0},{192,64},{1,129},{65,193},{129,1},{193,65... | collective-permute-start | bytes 552968 | tf_op jit(solution)/shard_map/ppermute | solution.py:401
  120.5 6.1 %collective-permute-start.4 = (bf16[128,720]{0,1:T(8,128)(2,1)S(1)}, bf16[128,720]{0,1:T(8,128)(2,1)S(1)}, u32[]{:S(2)}, u32[]{:S(2)}) collective-permute-start(bf16[128,720]{0,1:T(8,128)(2,1)S(1)} %convolution_convert_fusion.5), channel_id=1, source_target_pairs={{0,192},{64,0},{128,64},{192,128},{1,193},{65,1},{129,65},{193,129... | collective-permute-start | bytes 552968 | tf_op jit(solution)/shard_map/ppermute | solution.py:401

commit v2 on v1

--- a/solution.py
+++ b/solution.py
@@ -21,10 +21,6 @@
 
 def segment_number(seg_ends, positions):
     return jnp.sum((positions[:, None] >= seg_ends[None, :]).astype(jnp.int32), axis=1)
-
-
-def pick(matrix, rows):
-    return jnp.dot(matrix, rows, preferred_element_type=f32).astype(bf16)
 
 
 def relation(index, cores, ys, zs):
@@ -327,6 +323,279 @@
     )(dispatch, normed, residual, combine, own_in, near_in, own_out)
 
 
+PIECE = 384
+PIECES = 8
+
+
+def attention_kernel(
+    grid,
+    sender,
+    place,
+    stream_t,
+    query,
+    key_value,
+    visible,
+    weight_hbm,
+    residual,
+    normed,
+    weight_t,
+    shuffle,
+    stack,
+    early_out,
+    early_in,
+    late_out,
+    late_in,
+    sorted_rows,
+    section,
+    context,
+    parts,
+    columns,
+    local_sem,
+    early_send,
+    early_recv,
+    late_send,
+    late_recv,
+    key_send,
+    key_recv,
+    context_send,
+    context_recv,
+    column_send,
+    column_recv,
+):
+    cores, ys, zs = grid
+    x = lax.axis_index("dp")
+    e = lax.axis_index("expert")
+    count = cores * ys * zs
+    rows = sender.shape[0]
+    share = rows // count
+    width = residual.shape[1]
+    slab = PIECES * share
+    mesh_id = pl.DeviceIdType.MESH
+
+    def remote(src, dst, ssem, rsem, device):
+        return pltpu.make_async_remote_copy(
+            src_ref=src, dst_ref=dst, send_sem=ssem, recv_sem=rsem, device_id=device, device_id_type=mesh_id
+        )
+
+    barrier = pltpu.get_barrier_semaphore()
+
+    def greet(step, carry):
+        pl.semaphore_signal(barrier, inc=1, device_id=(x, (e + step) % count), device_id_type=mesh_id)
+        return carry
+
+    lax.fori_loop(1, count, greet, 0)
+    for s in range(1, 4):
+        pl.semaphore_signal(barrier, inc=1, device_id=((x + s) % 4, e), device_id_type=mesh_id)
+    load = pltpu.make_async_copy(weight_hbm, weight_t, local_sem)
+    load.start()
+
+    size = count * slab
+    row = lax.broadcasted_iota(jnp.int32, (size, 1), 0)
+    column = lax.broadcasted_iota(jnp.int32, (size, size), 1)
+    source = (row % slab) // share * rows + row // slab * share + row % share
+    shuffle[0] = (column == source).astype(f32).astype(bf16)
+    source = (row % rows) // share * slab + row // rows * share + row % share
+    shuffle[1] = (column == source).astype(f32).astype(bf16)
+
+    def pack(values, out):
+        stack[...] = jnp.zeros_like(stack)
+        for start, value in values:
+            done = 0
+            while done < value.shape[1]:
+                piece, offset = (start + done) // PIECE, (start + done) % PIECE
+                part = min(PIECE - offset, value.shape[1] - done)
+                stack[pl.ds(piece * rows, rows), pl.ds(offset, part)] = value[:, done : done + part]
+                done += part
+        out[...] = (
+            jnp.dot(shuffle[0], stack[...], preferred_element_type=f32).astype(bf16).reshape(count, slab, PIECE)
+        )
+
+    def unpack(got):
+        stack[...] = jnp.dot(
+            shuffle[1], got[...].reshape(size, PIECE), preferred_element_type=f32
+        ).astype(bf16)
+
+    def send_all(src, dst, ssem, rsem):
+        def one(index, carry):
+            remote(src.at[index], dst.at[index], ssem, rsem, (x, peer(e, index, 1, cores, ys, zs))).start()
+            return carry
+
+        lax.fori_loop(1, count, one, 0)
+        dst[0] = src[0]
+
+    def all_of(src, dst, ssem, rsem):
+        return remote(src.at[pl.ds(1, count - 1)], dst.at[pl.ds(1, count - 1)], ssem, rsem, (x, (e + 1) % count))
+
+    query_width, memory_width = query.shape[1], key_value.shape[1]
+    early_width = query_width + memory_width
+    pack(
+        [
+            (0, jnp.dot(sender[...], query[...], preferred_element_type=f32).astype(bf16)),
+            (query_width, jnp.dot(sender[...], key_value[...], preferred_element_type=f32).astype(bf16)),
+            (early_width, jnp.dot(sender[...], place[...], preferred_element_type=f32).astype(bf16)),
+        ],
+        early_out,
+    )
+    pl.semaphore_wait(barrier, count + 2)
+    send_all(early_out, early_in, early_send, early_recv)
+    pack(
+        [
+            (
+                0,
+                lax.dot_general(
+                    sender[...], stream_t[...], (((1,), (1,)), ((), ())), preferred_element_type=f32
+                ).astype(bf16),
+            )
+        ],
+        late_out,
+    )
+    send_all(late_out, late_in, late_send, late_recv)
+
+    all_of(early_out, early_in, early_send, early_recv).wait_recv()
+    unpack(early_in)
+    last, offset = early_width // PIECE, early_width % PIECE
+    spots = stack[pl.ds(last * rows, rows), pl.ds(offset, 128)].astype(f32)
+    settle = jnp.transpose(spots)[:rows].astype(bf16)
+    for piece in range(last + 1):
+        part = min(PIECE, early_width - piece * PIECE)
+        moved = jnp.dot(settle, stack[pl.ds(piece * rows, rows), :], preferred_element_type=f32).astype(bf16)
+        sorted_rows[:, pl.ds(piece * PIECE, part)] = moved[:, :part]
+    section[0] = sorted_rows[:, pl.ds(query_width, memory_width)]
+    for s in range(1, 4):
+        remote(section.at[0], section.at[s], key_send, key_recv, ((x + s) % 4, e)).start()
+
+    keys = remote(section.at[pl.ds(1, 3)], section.at[pl.ds(1, 3)], key_send, key_recv, ((x + 1) % 4, e))
+    keys.wait_recv()
+    key_count = 4 * rows
+    group = HEADS // KV_HEADS
+    key_width = KV_HEADS * HEAD_DIM
+    for h in range(KV_HEADS):
+        key = section[:, :, h * HEAD_DIM : (h + 1) * HEAD_DIM].reshape(key_count, HEAD_DIM)
+        value = section[:, :, key_width + h * HEAD_DIM : key_width + (h + 1) * HEAD_DIM].reshape(
+            key_count, HEAD_DIM
+        )
+        head_rows = jnp.concatenate(
+            [
+                sorted_rows[:, (h * group + g) * HEAD_DIM : (h * group + g + 1) * HEAD_DIM]
+                for g in range(group)
+            ],
+            axis=0,
+        )
+        scores = lax.dot_general(
+            head_rows, key, (((1,), (1,)), ((), ())), preferred_element_type=f32
+        ) * HEAD_DIM ** (-0.5)
+        seen = (visible[...] > 0.0)[None]
+        scores = jnp.where(seen, scores.reshape(group, rows, key_count), masked_score)
+        top = jnp.max(scores, axis=-1, keepdims=True)
+        weights = jnp.where(seen, jnp.exp(scores - top), 0.0)
+        denominator = jnp.sum(weights, axis=-1, keepdims=True)
+        numerator = jnp.dot(
+            weights.astype(bf16).reshape(group * rows, key_count), value, preferred_element_type=f32
+        ).reshape(group, rows, HEAD_DIM)
+        heads = (numerator / denominator).astype(bf16)
+        context[0, h] = jnp.concatenate([heads[g] for g in range(group)], axis=1)
+        for s in (2, 1, 3):
+            remote(
+                context.at[0, h], context.at[s, h], context_send.at[s - 1], context_recv.at[s - 1], ((x + s) % 4, e)
+            ).start()
+
+    load.wait()
+    depth = group * HEAD_DIM
+
+    def project(s):
+        total = None
+        for h in range(KV_HEADS):
+            term = lax.dot_general(
+                context[s, h],
+                weight_t[:, pl.ds(h * depth, depth)],
+                (((1,), (1,)), ((), ())),
+                preferred_element_type=f32,
+            )
+            total = term if total is None else total + term
+        return total.astype(bf16)
+
+    def whole_context(s):
+        return remote(
+            context.at[0], context.at[s], context_send.at[s - 1], context_recv.at[s - 1], ((x + s) % 4, e)
+        )
+
+    columns[x] = project(0)
+    all_of(late_out, late_in, late_send, late_recv).wait_recv()
+    unpack(late_in)
+    for start in range(0, width, PIECE):
+        part = min(PIECE, width - start)
+        moved = jnp.dot(
+            settle, stack[pl.ds(start // PIECE * rows, rows), :], preferred_element_type=f32
+        )
+        residual[:, pl.ds(start, part)] = moved[:, :part]
+    for s in (1, 3, 2):
+        whole_context(s).wait_recv()
+        parts[s - 1] = project(s)
+        remote(parts.at[s - 1], columns.at[x], column_send, column_recv, ((x + 4 - s) % 4, e)).start()
+    done = remote(parts, columns.at[pl.ds(0, 3)], column_send, column_recv, ((x + 1) % 4, e))
+    done.wait_recv()
+    update = jnp.concatenate([columns[d] for d in range(4)], axis=1).astype(f32)
+    total = residual[...] + update
+    residual[...] = total
+    scale = lax.rsqrt(jnp.mean(total * total, axis=-1, keepdims=True) + norm_eps)
+    normed[...] = (total * scale).astype(bf16)
+    done.wait_send()
+    keys.wait_send()
+    for s in range(1, 4):
+        whole_context(s).wait_send()
+    all_of(early_out, early_in, early_send, early_recv).wait_send()
+    all_of(late_out, late_in, late_send, late_recv).wait_send()
+
+
+def attend(grid, sender, place, stream_t, query, key_value, visible, weight_t):
+    rows = sender.shape[0]
+    width = stream_t.shape[0]
+    count = grid[0] * grid[1] * grid[2]
+    slab = PIECES * (rows // count)
+    size = count * slab
+    vmem = pl.BlockSpec(memory_space=pltpu.VMEM)
+    hbm = pl.BlockSpec(memory_space=pl.ANY)
+    dma = pltpu.SemaphoreType.DMA
+    slabs = pltpu.VMEM((count, slab, PIECE), bf16)
+    early_width = query.shape[1] + key_value.shape[1]
+    return pl.pallas_call(
+        functools.partial(attention_kernel, grid),
+        out_shape=[jax.ShapeDtypeStruct((rows, width), f32), jax.ShapeDtypeStruct((rows, width), bf16)],
+        in_specs=[vmem] * 6 + [hbm],
+        out_specs=[vmem, vmem],
+        scratch_shapes=[
+            pltpu.VMEM(weight_t.shape, bf16),
+            pltpu.VMEM((2, size, size), bf16),
+            pltpu.VMEM((size, PIECE), bf16),
+            slabs,
+            slabs,
+            slabs,
+            slabs,
+            pltpu.VMEM((rows, early_width), bf16),
+            pltpu.VMEM((4, rows, key_value.shape[1]), bf16),
+            pltpu.VMEM((4, KV_HEADS, rows, HEADS // KV_HEADS * HEAD_DIM), bf16),
+            pltpu.VMEM((3, rows, width // 4), bf16),
+            pltpu.VMEM((4, rows, width // 4), bf16),
+            dma,
+            dma,
+            dma,
+            dma,
+            dma,
+            dma,
+            dma,
+            dma((3,)),
+            dma((3,)),
+            dma,
+            dma,
+        ],
+        compiler_params=pltpu.CompilerParams(
+            collective_id=2, has_side_effects=True, vmem_limit_bytes=60 << 20
+        ),
+        cost_estimate=pl.CostEstimate(flops=5 << 30, bytes_accessed=8 << 20, transcendentals=0),
+        name="attend",
+    )(sender, place, stream_t, query, key_value, visible, weight_t)
+
+
 def on_device(
     stream_rows,
     query_rows,
@@ -363,80 +632,25 @@
         ((pack[:, None] == pack[None, :]) & (row_id[None, :] < row_id[:, None])).astype(jnp.int32), axis=1
     )
     send_slot = pack * share + rank
-    sender = (row_id[:, None] == send_slot[None, :]).astype(bf16)
-    place = jnp.broadcast_to((destination % row_count).astype(bf16)[:, None], (row_count, 128))
-    attention_rows = jnp.concatenate([query_rows, key_value_rows, place], axis=1)
-    query_width = query_rows.shape[1]
-    memory_width = key_value_rows.shape[1]
-
-    def exchange(rows):
-        width = rows.shape[1]
-        moved = lax.all_to_all(
-            pick(sender, rows).reshape(expert_count, share, width),
-            "expert",
-            split_axis=0,
-            concat_axis=0,
-            tiled=True,
-        )
-        return moved.reshape(row_count, width)
-
-    got = exchange(attention_rows)
-    got_stream = exchange(stream_rows)
-    place_got = got[:, query_width + memory_width].astype(jnp.int32)
-    settle = (row_id[:, None] == place_got[None, :]).astype(bf16)
-    memory = pick(settle, got[:, query_width : query_width + memory_width])
-    queries = pick(settle, got[:, :query_width])
-    stream = jnp.dot(settle, got_stream, preferred_element_type=f32)
-
-    group_size = HEADS // KV_HEADS
-    key_width = KV_HEADS * HEAD_DIM
+    slab = jnp.arange(expert_count, dtype=jnp.int32)
+    holder = peer(lax.axis_index("expert"), slab, 1, *grid)
+    slot_of = jnp.repeat(holder, share) * share + jnp.tile(jnp.arange(share, dtype=jnp.int32), expert_count)
+    sender = (slot_of[:, None] == send_slot[None, :]).astype(bf16)
+    lane = jnp.arange(128, dtype=jnp.int32)
+    place = ((destination % row_count)[:, None] == lane[None, :]).astype(bf16)
     seg_ends = jnp.cumsum(lengths[0])[:-1]
     query_position = my_block * row_count + row_id
     query_segment = segment_number(seg_ends, query_position)
-    query_heads = queries.reshape(row_count, KV_HEADS, group_size, HEAD_DIM)
-
-    def shift(value, step):
-        if step == 0:
-            return value
-        return lax.ppermute(value, "dp", [(x, (x + step) % dp_count) for x in range(dp_count)])
-
-    section = jnp.concatenate([shift(memory, s) for s in range(dp_count)], axis=0)
     key_position = jnp.concatenate(
         [lax.rem(my_block - s + dp_count, dp_count) * row_count + row_id for s in range(dp_count)]
     )
-    key_count = section.shape[0]
     key_segment = segment_number(seg_ends, key_position)
     visible = (query_segment[:, None] == key_segment[None, :]) & (
         key_position[None, :] <= query_position[:, None]
     )
-    key_block = section[:, :key_width].reshape(key_count, KV_HEADS, HEAD_DIM)
-    value_block = section[:, key_width:].reshape(key_count, KV_HEADS, HEAD_DIM)
-    scores = jnp.einsum(
-        "tkgd,nkd->kgtn", query_heads, key_block, preferred_element_type=f32
-    ) * HEAD_DIM ** (-0.5)
-    scores = jnp.where(visible, scores, masked_score)
-    row_max = jnp.max(scores, axis=-1)
-    weights = jnp.where(visible, jnp.exp(scores - row_max[..., None]), 0.0)
-    denominator = jnp.sum(weights, axis=-1)
-    numerator = jnp.einsum(
-        "kgtn,nkd->kgtd", weights.astype(bf16), value_block, preferred_element_type=f32
-    )
-    context = (
-        (numerator / denominator[..., None])
-        .transpose(2, 0, 1, 3)
-        .reshape(row_count, HEADS * HEAD_DIM)
-        .astype(bf16)
-    )
-    parts = []
-    for s in range(dp_count):
-        part = jnp.dot(shift(context, s), out_weight, preferred_element_type=f32).astype(bf16)
-        parts.append(shift(part, (dp_count - s) % dp_count))
-    order = lax.rem(jnp.arange(dp_count, dtype=jnp.int32) - my_block + dp_count, dp_count)
-    update = jnp.stack(parts)[order].transpose(1, 0, 2).reshape(row_count, model_width)
-    residual = stream + update.astype(f32)
-    normed = (
-        residual * lax.rsqrt(jnp.mean(residual * residual, axis=-1, keepdims=True) + norm_eps)
-    ).astype(bf16)
+    residual, normed = attend(
+        grid, sender, place, stream_rows.T, query_rows, key_value_rows, visible.astype(f32), out_weight.T
+    )
 
     entry_count = row_count * TOPK
     capacity = entry_count // expert_count
@@ -447,8 +661,6 @@
     slot_index = jnp.sum(onehot * (jnp.cumsum(onehot, axis=0) - 1), axis=1)
     kept_mask = slot_index < capacity
     slots = expert_count * capacity
-    slab = jnp.arange(expert_count, dtype=jnp.int32)
-    holder = peer(lax.axis_index("expert"), slab, 1, *grid)
     slab_expert = jnp.repeat(holder, capacity)
     slab_slot = jnp.tile(jnp.arange(capacity, dtype=jnp.int32), expert_count)
     slot_id = slab_expert * capacity + slab_slot

time: 288 us -> 246 us (0.85)
  Pallas kernels: 145 us -> 230 us
  waiting for transfers between devices: 43.7 us -> 0.01 us
  starting transfers between devices: 34.1 us -> 3.31 us
  matrix products: 26.8 us -> 0 us
  local copies, waits for them, and re-layouts: 25.6 us -> 4.91 us
  other arithmetic: 11.4 us -> 7.42 us
    pallas_call x0 -> x1, Pallas kernels: none -> 80.3 us  [attend(): pl.pallas_call(functools.partial(attention_kernel, grid), out_shape=[jax....]
    ppermute x9 -> x0, waiting for transfers between devices: 37.1 us -> none  [shift(): lax.ppermute(value, 'dp', [(x, (x + step) % dp_count) for x in range(dp_c...]
    dot_general x10 -> x0, matrix products: 20.1 us -> none  [the longest x4 7.7 us: pick(): return jnp.dot(matrix, rows, preferred_element_type=f32).astype(bf16)]
    all_to_all x2 -> x0, starting transfers between devices: 19.4 us -> none  [exchange(): lax.all_to_all(pick(sender, rows).reshape(expert_count, share, width), 'e...]
    ppermute x9 -> x0, starting transfers between devices: 12.1 us -> none  [shift(): lax.ppermute(value, 'dp', [(x, (x + step) % dp_count) for x in range(dp_c...]
    reshape x4 -> x0, local copies, waits for them, and re-layouts: 11.1 us -> none  [the longest x2 5.67 us: exchange(): return moved.reshape(row_count, width)]
    sub x1 -> x0, matrix products: 6.64 us -> none  [on_device(): weights = jnp.where(visible, jnp.exp(scores - row_max[..., None]), 0.0)]
    all_to_all x2 -> x0, waiting for transfers between devices: 6.62 us -> none  [exchange(): lax.all_to_all(pick(sender, rows).reshape(expert_count, share, width), 'e...]
  transfers between devices with their start and end apart: 12 -> 1, of which waited for: 5 -> 0; matrix products, arithmetic and copies ran while one was open for 19% -> 4% of each run, Pallas kernels for 0% -> 33%
where the time goes in v2:
time: 246 us; the launch traced here: 245 us
  Pallas kernels  230 us (93%)
  other arithmetic  7.42 us (3%)
  local copies, waits for them, and re-layouts  4.91 us (2%)
  starting transfers between devices  3.31 us (1%)
    pallas_call x1, Pallas kernels, experts(): pl.pallas_call(functools.partial(expert_kernel, grid), out_shape=jax.Shap...  149 us
    pallas_call x1, Pallas kernels, attend(): pl.pallas_call(functools.partial(attention_kernel, grid), out_shape=[jax....  80.3 us
  transfers between devices with their start and end apart: 1, of which 0 were waited for; matrix products, arithmetic and copies ran while one was open for 4% of the time, Pallas kernels for 33%

profile of v2, /device:TPU:1, one launch (start us, length us, event | category | flops | bytes accessed | tf_op | source)
XLA Modules:
  0.0 245.4 jit_solution(11079676823248327491)
XLA Ops:
  0.0 3.3 %collective-permute-start = (bf16[720,2880]{1,0:T(8,128)(2,1)}, bf16[720,2880]{1,0:T(8,128)(2,1)}, u32[]{:S(2)}, u32[]{:S(2)}) collective-permute-start(bf16[720,2880]{1,0:T(8,128)(2,1)} %bitcast.40), channel_id=1, source_target_pairs={{0,64},{1,193},{2,66},{3,195},{4,68},{5,197},{6,70},{7,199},{8,72}... | collective-permute-start | bytes 12441608 | tf_op jit(solution)/shard_map/ppermute | solution.py:626
  3.3 0.8 copy.22
  4.1 0.1 eq.239
  4.2 0.1 eq.235
  4.3 0.8 reduce-window.14
  5.3 0.1 add.278
  5.5 0.1 add.284
  5.6 1.2 reduce-window.10
  6.8 0.2 slice_reduce_fusion
  7.1 0.1 fusion.2
  7.2 0.1 reduce_sum.39
  7.6 0.7 and_select_fusion
  8.3 0.2 convert_reduce_fusion
  8.5 0.2 slice_reduce_fusion.4
  8.7 0.8 slice_bitcast_fusion.3
  9.5 0.2 reduce-precision_convert_fusion
  9.8 0.7 pad_maximum_fusion.combine
  10.5 0.7 fusion.6.place
  11.2 0.7 compare_convert_fusion.sender
  11.9 0.8 add_convert_fusion.dispatch
  12.7 0.8 and_convert_fusion.visible
  13.5 80.3 %attend.1 = (f32[128,2880]{1,0:T(8,128)}, bf16[128,2880]{1,0:T(8,128)(2,1)}) custom-call(bf16[128,128]{1,0:T(8,128)(2,1)} %compare_convert_fusion.sender, bf16[128,128]{1,0:T(8,128)(2,1)} %fusion.6.place, bf16[2880,128]{1,0:T(8,128)(2,1)} %bitcast.44, bf16[128,2048]{1,0:T(8,128)(2,1)} %query.1, bf16[128,512]{1,0:T(8,128)(2,1)} %key_value.1, ...), custom_call_target="tpu_custom_call" | custom-call | flops 5368709120 | bytes 8388608 | tf_op jit(solution)/shard_map/attend/pallas_call | solution.py:561
  93.8 149.3 %experts.1 = bf16[128,2880]{1,0:T(8,128)(2,1)} custom-call(bf16[512,128]{1,0:T(8,128)(2,1)} %add_convert_fusion.dispatch, bf16[128,2880]{1,0:T(8,128)(2,1)} %get-tuple-element.7.normed, f32[128,2880]{1,0:T(8,128)} %get-tuple-element.8.residual, bf16[2,128,512]{2,1,0:T(8,128)(2,1)} %pad_maximum_fusion.combine, bf16[720,2880]{1,0:T(8,128)(2,1)} %bitcast.41, ...), custom_call_target="tpu_custom_call" | custom-call | flops 15032385536 | bytes 31457280 | tf_op jit(solution)/shard_map/experts/pallas_call | solution.py:297
  243.1 2.3 copy.26
  (16 shorter events, 0.5 us)
Async XLA Ops:
  0.0 93.8 %collective-permute-start = (bf16[720,2880]{1,0:T(8,128)(2,1)}, bf16[720,2880]{1,0:T(8,128)(2,1)}, u32[]{:S(2)}, u32[]{:S(2)}) collective-permute-start(bf16[720,2880]{1,0:T(8,128)(2,1)} %bitcast.40), channel_id=1, source_target_pairs={{0,64},{1,193},{2,66},{3,195},{4,68},{5,197},{6,70},{7,199},{8,72}... | collective-permute-start | bytes 12441608 | tf_op jit(solution)/shard_map/ppermute | solution.py:626

commit v3 on v2

--- a/solution.py
+++ b/solution.py
@@ -17,10 +17,6 @@
 norm_eps = 1e-05
 f32 = jnp.float32
 bf16 = jnp.bfloat16
-
-
-def segment_number(seg_ends, positions):
-    return jnp.sum((positions[:, None] >= seg_ends[None, :]).astype(jnp.int32), axis=1)
 
 
 def relation(index, cores, ys, zs):
@@ -110,12 +106,15 @@
         )
 
     load_own = pltpu.make_async_copy(own_in, raw_in.at[0], local_sem.at[0])
-    load_near = pltpu.make_async_copy(near_in, raw_in.at[1], local_sem.at[1])
+    load_near = pltpu.make_async_copy(near_in, raw_in.at[1, pl.ds(0, near_in.shape[0])], local_sem.at[1])
     load_out = pltpu.make_async_copy(own_out, raw_out.at[0], local_sem.at[2])
     load_own.start()
     load_near.start()
     load_out.start()
-    weight_out = remote(own_out, raw_out.at[1], weight_send, weight_recv, pair)
+    sent = near_in.shape[0]
+    rest = pl.ds(sent, columns - sent)
+    weight_in = remote(own_in.at[rest], raw_in.at[1, rest], weight_send.at[0], weight_recv.at[0], pair)
+    weight_out = remote(own_out, raw_out.at[1], weight_send.at[1], weight_recv.at[1], pair)
 
     def chunk_of(ref, c):
         return ref.at[pl.ds(c * per, per)]
@@ -142,6 +141,7 @@
     pack_dispatch(0)
     pl.semaphore_wait(barrier, count + 1)
     send_dispatch(0)
+    weight_in.start()
     weight_out.start()
     lax.fori_loop(1, 4, begin, 0)
     in_own[0] = out_buf[0]
@@ -160,7 +160,6 @@
     load_own.wait()
     separate(0)
     load_near.wait()
-    separate(1)
     load_out.wait()
 
     def wait_own(c):
@@ -236,6 +235,8 @@
 
         @pl.when(t == 1)
         def _():
+            weight_in.wait()
+            separate(1)
             weight_out.wait()
 
         @pl.when((t >= 1) & (t < 5))
@@ -313,8 +314,8 @@
             buffer,
             buffer,
             dma((3,)),
-            dma,
-            dma,
+            dma((2,)),
+            dma((2,)),
         ]
         + [dma((4,))] * 8,
         compiler_params=pltpu.CompilerParams(collective_id=1, has_side_effects=True, vmem_limit_bytes=60 << 20),
@@ -329,15 +330,20 @@
 
 def attention_kernel(
     grid,
-    sender,
-    place,
+    destination,
+    lengths,
+    expert_index,
+    router_weights,
     stream_t,
     query,
     key_value,
-    visible,
     weight_hbm,
+    own_in,
     residual,
     normed,
+    dispatch,
+    combine,
+    near_in,
     weight_t,
     shuffle,
     stack,
@@ -351,6 +357,8 @@
     parts,
     columns,
     local_sem,
+    near_send,
+    near_recv,
     early_send,
     early_recv,
     late_send,
@@ -366,7 +374,7 @@
     x = lax.axis_index("dp")
     e = lax.axis_index("expert")
     count = cores * ys * zs
-    rows = sender.shape[0]
+    rows = destination.shape[1]
     share = rows // count
     width = residual.shape[1]
     slab = PIECES * share
@@ -426,30 +434,70 @@
     def all_of(src, dst, ssem, rsem):
         return remote(src.at[pl.ds(1, count - 1)], dst.at[pl.ds(1, count - 1)], ssem, rsem, (x, (e + 1) % count))
 
+    across = lax.broadcasted_iota(jnp.int32, (rows, rows), 1)
+    down = lax.broadcasted_iota(jnp.int32, (rows, rows), 0)
+    target_row = jnp.broadcast_to(destination[...], (rows, rows))
+    target_col = jnp.sum(jnp.where(across == down, target_row, 0), axis=1, keepdims=True)
+    bits = (4 * rows).bit_length() - 1
+    pack_row = lax.shift_right_logical(target_row, bits)
+    pack_col = lax.shift_right_logical(target_col, bits)
+    rank = jnp.sum(((pack_row == pack_col) & (down < across)).astype(jnp.int32), axis=0, keepdims=True)
+    index = lax.broadcasted_iota(jnp.int32, (rows, 1), 0)
+    slot = peer(e, index // share, 1, cores, ys, zs) * share + index % share
+    sender = (slot == pack_row * share + rank).astype(f32).astype(bf16)
+    lane = lax.broadcasted_iota(jnp.int32, (rows, 128), 1)
+    place = (lane == (target_col & (rows - 1))).astype(f32).astype(bf16)
+
     query_width, memory_width = query.shape[1], key_value.shape[1]
     early_width = query_width + memory_width
     pack(
         [
-            (0, jnp.dot(sender[...], query[...], preferred_element_type=f32).astype(bf16)),
-            (query_width, jnp.dot(sender[...], key_value[...], preferred_element_type=f32).astype(bf16)),
-            (early_width, jnp.dot(sender[...], place[...], preferred_element_type=f32).astype(bf16)),
+            (0, jnp.dot(sender, query[...], preferred_element_type=f32).astype(bf16)),
+            (query_width, jnp.dot(sender, key_value[...], preferred_element_type=f32).astype(bf16)),
+            (early_width, jnp.dot(sender, place, preferred_element_type=f32).astype(bf16)),
         ],
         early_out,
     )
     pl.semaphore_wait(barrier, count + 2)
+    near = remote(
+        own_in.at[pl.ds(0, near_in.shape[0])], near_in, near_send, near_recv, (weight_pair(x, e % cores), e)
+    )
+    near.start()
     send_all(early_out, early_in, early_send, early_recv)
     pack(
         [
             (
                 0,
                 lax.dot_general(
-                    sender[...], stream_t[...], (((1,), (1,)), ((), ())), preferred_element_type=f32
+                    sender, stream_t[...], (((1,), (1,)), ((), ())), preferred_element_type=f32
                 ).astype(bf16),
             )
         ],
         late_out,
     )
     send_all(late_out, late_in, late_send, late_recv)
+
+    slots, capacity = dispatch.shape[0], dispatch.shape[0] // count
+    holder = peer(e, lax.broadcasted_iota(jnp.int32, (count, 1), 0), 1, cores, ys, zs)
+    chosen = jnp.zeros((count, rows), f32)
+    weight = jnp.zeros((count, rows), f32)
+    for k in range(TOPK):
+        match = holder == expert_index[k : k + 1, :]
+        chosen += match.astype(f32)
+        weight += jnp.where(match, router_weights[k : k + 1, :], 0.0)
+    before = (down < across).astype(f32).astype(bf16)
+    earlier = jnp.dot(chosen.astype(bf16), before, preferred_element_type=f32)
+    earlier = jnp.where(chosen > 0.0, earlier, -1.0)
+    slot_row = lax.broadcasted_iota(jnp.int32, (slots, count), 0)
+    spread = (slot_row // capacity == lax.broadcasted_iota(jnp.int32, (slots, count), 1)).astype(f32).astype(bf16)
+    number = (lax.broadcasted_iota(jnp.int32, (slots, rows), 0) % capacity).astype(f32)
+    taken = jnp.dot(spread, earlier.astype(bf16), preferred_element_type=f32) == number
+    dispatch[...] = taken.astype(f32).astype(bf16)
+    high = weight.astype(bf16)
+    low = (weight - high.astype(f32)).astype(bf16)
+    for i, value in enumerate((high, low)):
+        wide = jnp.dot(spread, value, preferred_element_type=f32)
+        combine[i] = jnp.transpose(jnp.where(taken, wide, 0.0)).astype(bf16)
 
     all_of(early_out, early_in, early_send, early_recv).wait_recv()
     unpack(early_in)
@@ -469,6 +517,15 @@
     key_count = 4 * rows
     group = HEADS // KV_HEADS
     key_width = KV_HEADS * HEAD_DIM
+    first, second = lengths[0, 0], lengths[0, 0] + lengths[0, 1]
+
+    def segment(position):
+        return (position >= first).astype(jnp.int32) + (position >= second).astype(jnp.int32)
+
+    key_lane = lax.broadcasted_iota(jnp.int32, (rows, key_count), 1)
+    key_place = (x + 4 - key_lane // rows) % 4 * rows + key_lane % rows
+    query_place = x * rows + lax.broadcasted_iota(jnp.int32, (rows, key_count), 0)
+    seen = ((segment(key_place) == segment(query_place)) & (key_place <= query_place))[None]
     for h in range(KV_HEADS):
         key = section[:, :, h * HEAD_DIM : (h + 1) * HEAD_DIM].reshape(key_count, HEAD_DIM)
         value = section[:, :, key_width + h * HEAD_DIM : key_width + (h + 1) * HEAD_DIM].reshape(
@@ -484,7 +541,6 @@
         scores = lax.dot_general(
             head_rows, key, (((1,), (1,)), ((), ())), preferred_element_type=f32
         ) * HEAD_DIM ** (-0.5)
-        seen = (visible[...] > 0.0)[None]
         scores = jnp.where(seen, scores.reshape(group, rows, key_count), masked_score)
         top = jnp.max(scores, axis=-1, keepdims=True)
         weights = jnp.where(seen, jnp.exp(scores - top), 0.0)
@@ -540,6 +596,7 @@
     scale = lax.rsqrt(jnp.mean(total * total, axis=-1, keepdims=True) + norm_eps)
     normed[...] = (total * scale).astype(bf16)
     done.wait_send()
+    near.wait()
     keys.wait_send()
     for s in range(1, 4):
         whole_context(s).wait_send()
@@ -547,12 +604,13 @@
     all_of(late_out, late_in, late_send, late_recv).wait_send()
 
 
-def attend(grid, sender, place, stream_t, query, key_value, visible, weight_t):
-    rows = sender.shape[0]
+def attend(grid, sent, destination, lengths, expert_index, router_weights, stream_t, query, key_value, weight_t, own_in):
+    rows = destination.shape[1]
     width = stream_t.shape[0]
     count = grid[0] * grid[1] * grid[2]
     slab = PIECES * (rows // count)
     size = count * slab
+    slots = rows * TOPK
     vmem = pl.BlockSpec(memory_space=pltpu.VMEM)
     hbm = pl.BlockSpec(memory_space=pl.ANY)
     dma = pltpu.SemaphoreType.DMA
@@ -560,9 +618,15 @@
     early_width = query.shape[1] + key_value.shape[1]
     return pl.pallas_call(
         functools.partial(attention_kernel, grid),
-        out_shape=[jax.ShapeDtypeStruct((rows, width), f32), jax.ShapeDtypeStruct((rows, width), bf16)],
-        in_specs=[vmem] * 6 + [hbm],
-        out_specs=[vmem, vmem],
+        out_shape=[
+            jax.ShapeDtypeStruct((rows, width), f32),
+            jax.ShapeDtypeStruct((rows, width), bf16),
+            jax.ShapeDtypeStruct((slots, rows), bf16),
+            jax.ShapeDtypeStruct((2, rows, slots), bf16),
+            jax.ShapeDtypeStruct((sent, width), bf16),
+        ],
+        in_specs=[vmem, pl.BlockSpec(memory_space=pltpu.SMEM)] + [vmem] * 5 + [hbm] * 2,
+        out_specs=[vmem] * 4 + [hbm],
         scratch_shapes=[
             pltpu.VMEM(weight_t.shape, bf16),
             pltpu.VMEM((2, size, size), bf16),
@@ -576,24 +640,16 @@
             pltpu.VMEM((4, KV_HEADS, rows, HEADS // KV_HEADS * HEAD_DIM), bf16),
             pltpu.VMEM((3, rows, width // 4), bf16),
             pltpu.VMEM((4, rows, width // 4), bf16),
-            dma,
-            dma,
-            dma,
-            dma,
-            dma,
-            dma,
-            dma,
-            dma((3,)),
-            dma((3,)),
-            dma,
-            dma,
-        ],
+        ]
+        + [dma] * 9
+        + [dma((3,))] * 2
+        + [dma] * 2,
         compiler_params=pltpu.CompilerParams(
             collective_id=2, has_side_effects=True, vmem_limit_bytes=60 << 20
         ),
         cost_estimate=pl.CostEstimate(flops=5 << 30, bytes_accessed=8 << 20, transcendentals=0),
         name="attend",
-    )(sender, place, stream_t, query, key_value, visible, weight_t)
+    )(destination, lengths, expert_index, router_weights, stream_t, query, key_value, weight_t, own_in)
 
 
 def on_device(
@@ -609,72 +665,25 @@
     down_weight,
 ):
     row_count, model_width = stream_rows.shape
-    dp_count = lax.axis_size("dp")
     expert_count = lax.axis_size("expert")
-    seq_len = row_count * dp_count
-    my_block = lax.axis_index("dp")
-    both = ("dp", "expert")
     cores, ys = 2, 4
     grid = (cores, ys, expert_count // (cores * ys))
     own_in = gate_up[0].T
-    own_out = down_weight[0]
-    swap = [
-        (d * expert_count + e, weight_pair(d, e % cores) * expert_count + e)
-        for d in range(dp_count)
-        for e in range(expert_count)
-    ]
-    near_in = lax.ppermute(own_in, ("dp", "expert"), swap)
-
-    share = row_count // expert_count
-    row_id = jnp.arange(row_count, dtype=jnp.int32)
-    pack = destination // seq_len
-    rank = jnp.sum(
-        ((pack[:, None] == pack[None, :]) & (row_id[None, :] < row_id[:, None])).astype(jnp.int32), axis=1
+    sent = own_in.shape[0] * 5 // 128 * 16
+    residual, normed, dispatch, combine, near_in = attend(
+        grid,
+        sent,
+        destination.reshape(1, row_count),
+        lengths,
+        expert_index[0].T,
+        router_weights[0].T,
+        stream_rows.T,
+        query_rows,
+        key_value_rows,
+        out_weight.T,
+        own_in,
     )
-    send_slot = pack * share + rank
-    slab = jnp.arange(expert_count, dtype=jnp.int32)
-    holder = peer(lax.axis_index("expert"), slab, 1, *grid)
-    slot_of = jnp.repeat(holder, share) * share + jnp.tile(jnp.arange(share, dtype=jnp.int32), expert_count)
-    sender = (slot_of[:, None] == send_slot[None, :]).astype(bf16)
-    lane = jnp.arange(128, dtype=jnp.int32)
-    place = ((destination % row_count)[:, None] == lane[None, :]).astype(bf16)
-    seg_ends = jnp.cumsum(lengths[0])[:-1]
-    query_position = my_block * row_count + row_id
-    query_segment = segment_number(seg_ends, query_position)
-    key_position = jnp.concatenate(
-        [lax.rem(my_block - s + dp_count, dp_count) * row_count + row_id for s in range(dp_count)]
-    )
-    key_segment = segment_number(seg_ends, key_position)
-    visible = (query_segment[:, None] == key_segment[None, :]) & (
-        key_position[None, :] <= query_position[:, None]
-    )
-    residual, normed = attend(
-        grid, sender, place, stream_rows.T, query_rows, key_value_rows, visible.astype(f32), out_weight.T
-    )
-
-    entry_count = row_count * TOPK
-    capacity = entry_count // expert_count
-    flat_index = expert_index.reshape(entry_count)
-    onehot = (flat_index[:, None] == jnp.arange(expert_count, dtype=jnp.int32)[None, :]).astype(
-        jnp.int32
-    )
-    slot_index = jnp.sum(onehot * (jnp.cumsum(onehot, axis=0) - 1), axis=1)
-    kept_mask = slot_index < capacity
-    slots = expert_count * capacity
-    slab_expert = jnp.repeat(holder, capacity)
-    slab_slot = jnp.tile(jnp.arange(capacity, dtype=jnp.int32), expert_count)
-    slot_id = slab_expert * capacity + slab_slot
-    target = jnp.where(kept_mask, flat_index * capacity + slot_index, slots).reshape(row_count, TOPK)
-    dispatch = jnp.zeros((slots, row_count), f32)
-    combine = jnp.zeros((row_count, slots), f32)
-    entry_weight = router_weights.reshape(row_count, TOPK)
-    for k in range(TOPK):
-        dispatch = dispatch + (slot_id[:, None] == target[None, :, k]).astype(f32)
-        combine = combine + jnp.where(target[:, k, None] == slot_id[None, :], entry_weight[:, k, None], 0.0)
-    high = lax.reduce_precision(combine, 8, 7)
-    low = (combine - high).astype(bf16)
-    combine = jnp.stack([high.astype(bf16), low])
-    scored = experts(grid, dispatch.astype(bf16), normed, residual, combine, own_in, near_in, own_out)
+    scored = experts(grid, dispatch, normed, residual, combine, own_in, near_in, down_weight[0])
     return scored.reshape(1, row_count, model_width)
 
 

time: 246 us -> 243 us (0.988)
  Pallas kernels: 230 us -> 239 us
  other arithmetic: 7.42 us -> 0 us
  starting transfers between devices: 3.31 us -> 0 us
  local copies, waits for them, and re-layouts: 4.91 us -> 2.26 us
    pallas_call x1, Pallas kernels: 80.3 us -> 91.9 us  [attend(): pl.pallas_call(functools.partial(attention_kernel, grid), out_shape=[jax....]
    ppermute x1 -> x0, starting transfers between devices: 3.31 us -> none  [on_device(): near_in = lax.ppermute(own_in, ('dp', 'expert'), swap)]
    convert_element_type x6 -> x0, other arithmetic: 3.24 us -> none  [the longest x1 0.82 us: on_device(): dispatch.astype(bf16)]
    another operation x4 -> x0, other arithmetic: 2.8 us -> none
    pallas_call x1, Pallas kernels: 149 us -> 147 us  [experts(): pl.pallas_call(functools.partial(expert_kernel, grid), out_shape=jax.Shap...]
  transfers between devices with their start and end apart: 1 -> 0, of which waited for: 0 -> 0; matrix products, arithmetic and copies ran while one was open for 4% -> 0% of each run, Pallas kernels for 33% -> 0%
where the time goes in v3:
time: 243 us; the launch traced here: 241 us
  Pallas kernels  239 us (98%)
    pallas_call x1, Pallas kernels, experts(): pl.pallas_call(functools.partial(expert_kernel, grid), out_shape=jax.Shap...  147 us
    pallas_call x1, Pallas kernels, attend(): pl.pallas_call(functools.partial(attention_kernel, grid), out_shape=[jax....  91.9 us

profile of v3, /device:TPU:1, one launch (start us, length us, event | category | flops | bytes accessed | tf_op | source)
XLA Modules:
  0.0 240.9 jit_solution(8435115953571272678)
XLA Ops:
  0.0 91.9 %attend.1 = (f32[128,2880]{1,0:T(8,128)}, bf16[128,2880]{1,0:T(8,128)(2,1)}, bf16[512,128]{1,0:T(8,128)(2,1)}, bf16[2,128,512]{2,1,0:T(8,128)(2,1)}, bf16[448,2880]{1,0:T(8,128)(2,1)}) custom-call(s32[1,128]{1,0:T(1,128)} %bitcast.22, s32[1,3]{1,0:T(1,128)} %lengths.1, s32[4,128]{1,0:T(4,128)} %bitcast.20, f32[4,128]{1,0:T(4,128)} %bitcast.21, ...), custom_call_target="tpu_custom_call" | custom-call | flops 5368709120 | bytes 8388608 | tf_op jit(solution)/shard_map/attend/pallas_call | solution.py:619
  91.9 146.7 %experts.1 = bf16[128,2880]{1,0:T(8,128)(2,1)} custom-call(bf16[512,128]{1,0:T(8,128)(2,1)} %get-tuple-element.10.dispatch, bf16[128,2880]{1,0:T(8,128)(2,1)} %get-tuple-element.11.normed, f32[128,2880]{1,0:T(8,128)} %get-tuple-element.12.residual, bf16[2,128,512]{2,1,0:T(8,128)(2,1)} %get-tuple-element.13.combine, bf16[720,2880]{1,0:T(8,128)(2,1)} %bitcast.16, ...), custom_call_target="tpu_custom_call" | custom-call | flops 15032385536 | bytes 31457280 | tf_op jit(solution)/shard_map/experts/pallas_call | solution.py:298
  238.6 2.3 copy.11

commit v4 on v3

--- a/solution.py
+++ b/solution.py
@@ -47,12 +47,14 @@
     normed,
     residual,
     combine,
+    near,
+    weight_in,
+    weight_out,
+    load_out,
     own_in,
-    near_in,
-    own_out,
     result,
     raw_in,
-    split_in,
+    split,
     raw_out,
     out_buf,
     in_own,
@@ -60,12 +62,9 @@
     x_buf,
     h_buf,
     own_part,
-    part_send,
     part_recv,
     ret_recv,
-    local_sem,
-    weight_send,
-    weight_recv,
+    own_sem,
     go_send,
     go_recv,
     twin_send,
@@ -78,43 +77,21 @@
     cores, ys, zs = grid
     x = lax.axis_index("dp")
     e = lax.axis_index("expert")
-    pair = (weight_pair(x, e % cores), e)
     twin = (weight_pair(x, 1 - e % cores), e)
     slabs, capacity, width = out_buf.shape
     per = slabs // 4
     rows = per * capacity
     columns = raw_in.shape[1]
     units = columns // 2
-    padded = split_in.shape[1] // 2
-    count = cores * ys * zs
-
-    barrier = pltpu.get_barrier_semaphore()
-
-    def greet(step, carry):
-        pl.semaphore_signal(
-            barrier, inc=1, device_id=(x, (e + step) % count), device_id_type=pl.DeviceIdType.MESH
-        )
-        return carry
-
-    lax.fori_loop(1, count, greet, 0)
-    pl.semaphore_signal(barrier, inc=1, device_id=pair, device_id_type=pl.DeviceIdType.MESH)
-    pl.semaphore_signal(barrier, inc=1, device_id=twin, device_id_type=pl.DeviceIdType.MESH)
+    padded = split.shape[0] // 4
 
     def remote(src, dst, ssem, rsem, device):
         return pltpu.make_async_remote_copy(
             src_ref=src, dst_ref=dst, send_sem=ssem, recv_sem=rsem, device_id=device, device_id_type=pl.DeviceIdType.MESH
         )
 
-    load_own = pltpu.make_async_copy(own_in, raw_in.at[0], local_sem.at[0])
-    load_near = pltpu.make_async_copy(near_in, raw_in.at[1, pl.ds(0, near_in.shape[0])], local_sem.at[1])
-    load_out = pltpu.make_async_copy(own_out, raw_out.at[0], local_sem.at[2])
+    load_own = pltpu.make_async_copy(own_in, raw_in.at[0], own_sem)
     load_own.start()
-    load_near.start()
-    load_out.start()
-    sent = near_in.shape[0]
-    rest = pl.ds(sent, columns - sent)
-    weight_in = remote(own_in.at[rest], raw_in.at[1, rest], weight_send.at[0], weight_recv.at[0], pair)
-    weight_out = remote(own_out, raw_out.at[1], weight_send.at[1], weight_recv.at[1], pair)
 
     def chunk_of(ref, c):
         return ref.at[pl.ds(c * per, per)]
@@ -138,12 +115,7 @@
         send_dispatch(c)
         return carry
 
-    pack_dispatch(0)
-    pl.semaphore_wait(barrier, count + 1)
-    send_dispatch(0)
-    weight_in.start()
-    weight_out.start()
-    lax.fori_loop(1, 4, begin, 0)
+    lax.fori_loop(0, 4, begin, 0)
     in_own[0] = out_buf[0]
 
     row = lax.broadcasted_iota(jnp.int32, (2 * padded, columns), 0)
@@ -155,12 +127,12 @@
     def separate(k):
         for start in range(0, width, 768):
             cols = pl.ds(start, min(768, width - start))
-            split_in[k, :, cols] = jnp.dot(part, raw_in[k, :, cols], preferred_element_type=f32).astype(bf16)
+            split[pl.ds(k * 2 * padded, 2 * padded), cols] = jnp.dot(part, raw_in[k, :, cols], preferred_element_type=f32).astype(bf16)
 
     load_own.wait()
     separate(0)
-    load_near.wait()
     load_out.wait()
+    near.wait()
 
     def wait_own(c):
         @pl.when(c == 0)
@@ -177,7 +149,7 @@
         return remote(chunk_of(in_own, c), chunk_of(in_twin, c), twin_send.at[c], twin_recv.at[c], twin)
 
     def partial(c):
-        return remote(chunk_of(part_send, c), chunk_of(part_recv, c), part_ssem.at[c], part_rsem.at[c], twin)
+        return remote(chunk_of(in_twin, c), chunk_of(part_recv, c), part_ssem.at[c], part_rsem.at[c], twin)
 
     def wait_sent(ref, sems, c):
         @pl.when(c == 0)
@@ -196,7 +168,9 @@
 
         def units_of(k, carry):
             projected = lax.dot_general(
-                x_buf[...], split_in[k], (((1,), (1,)), ((), ())), preferred_element_type=f32
+                x_buf[...],
+                split[pl.ds(pl.multiple_of(k * 2 * padded, 128), 2 * padded), :],
+                (((1,), (1,)), ((), ())), preferred_element_type=f32
             )
             gate = projected[:, :padded]
             up = projected[:, padded:]
@@ -210,12 +184,12 @@
             cols = pl.ds(start, size)
             total = jnp.dot(h_buf[0, :, :units], raw_out[0, :, cols], preferred_element_type=f32)
             total += jnp.dot(h_buf[1, :, :units], raw_out[1, :, cols], preferred_element_type=f32)
-            own_part[c, :, cols] = total[:rows]
-            part_send[pl.ds(c * per, per), :, cols] = total[rows:].astype(bf16).reshape(per, capacity, size)
+            own_part[c % 2, :, cols] = total[:rows]
+            in_twin[pl.ds(c * per, per), :, cols] = total[rows:].astype(bf16).reshape(per, capacity, size)
 
     def give_back(c):
         wait_sent(out_buf, go_send, c)
-        total = own_part[c] + part_recv[pl.ds(c * per, per)].astype(f32).reshape(rows, width)
+        total = own_part[c % 2] + part_recv[pl.ds(c * per, per)].astype(f32).reshape(rows, width)
         out_buf[pl.ds(c * per, per)] = total.astype(bf16).reshape(per, capacity, width)
 
         def one(m, carry):
@@ -280,48 +254,6 @@
         mixed = jnp.dot(combine[0], back, preferred_element_type=f32)
         mixed += jnp.dot(combine[1], back, preferred_element_type=f32)
         result[:, cols] = (residual[:, cols] + mixed).astype(bf16)
-
-
-def experts(grid, dispatch, normed, residual, combine, own_in, near_in, own_out):
-    slots, row_count = dispatch.shape
-    width = normed.shape[1]
-    columns = own_in.shape[0]
-    units = columns // 2
-    padded = -(-units // 128) * 128
-    slabs = grid[0] * grid[1] * grid[2]
-    capacity = slots // slabs
-    rows = slots // 4
-    vmem = pl.BlockSpec(memory_space=pltpu.VMEM)
-    hbm = pl.BlockSpec(memory_space=pl.ANY)
-    dma = pltpu.SemaphoreType.DMA
-    buffer = pltpu.VMEM((slabs, capacity, width), bf16)
-    return pl.pallas_call(
-        functools.partial(expert_kernel, grid),
-        out_shape=jax.ShapeDtypeStruct((row_count, width), bf16),
-        in_specs=[vmem, vmem, vmem, vmem, hbm, hbm, hbm],
-        out_specs=vmem,
-        scratch_shapes=[
-            pltpu.VMEM((2, columns, width), bf16),
-            pltpu.VMEM((2, 2 * padded, width), bf16),
-            pltpu.VMEM((2, units, width), bf16),
-            buffer,
-            buffer,
-            buffer,
-            pltpu.VMEM((2 * rows, width), bf16),
-            pltpu.VMEM((2, 2 * rows, padded), bf16),
-            pltpu.VMEM((4, rows, width), f32),
-            buffer,
-            buffer,
-            buffer,
-            dma((3,)),
-            dma((2,)),
-            dma((2,)),
-        ]
-        + [dma((4,))] * 8,
-        compiler_params=pltpu.CompilerParams(collective_id=1, has_side_effects=True, vmem_limit_bytes=60 << 20),
-        cost_estimate=pl.CostEstimate(flops=14 << 30, bytes_accessed=30 << 20, transcendentals=0),
-        name="experts",
-    )(dispatch, normed, residual, combine, own_in, near_in, own_out)
 
 
 PIECE = 384
@@ -338,12 +270,12 @@
     query,
     key_value,
     weight_hbm,
-    own_in,
+    near,
+    weight_rest,
     residual,
     normed,
     dispatch,
     combine,
-    near_in,
     weight_t,
     shuffle,
     stack,
@@ -357,8 +289,6 @@
     parts,
     columns,
     local_sem,
-    near_send,
-    near_recv,
     early_send,
     early_recv,
     late_send,
@@ -401,9 +331,9 @@
     row = lax.broadcasted_iota(jnp.int32, (size, 1), 0)
     column = lax.broadcasted_iota(jnp.int32, (size, size), 1)
     source = (row % slab) // share * rows + row // slab * share + row % share
-    shuffle[0] = (column == source).astype(f32).astype(bf16)
+    shuffle[0][...] = (column == source).astype(f32).astype(bf16)
     source = (row % rows) // share * slab + row // rows * share + row % share
-    shuffle[1] = (column == source).astype(f32).astype(bf16)
+    shuffle[1][...] = (column == source).astype(f32).astype(bf16)
 
     def pack(values, out):
         stack[...] = jnp.zeros_like(stack)
@@ -415,12 +345,12 @@
                 stack[pl.ds(piece * rows, rows), pl.ds(offset, part)] = value[:, done : done + part]
                 done += part
         out[...] = (
-            jnp.dot(shuffle[0], stack[...], preferred_element_type=f32).astype(bf16).reshape(count, slab, PIECE)
+            jnp.dot(shuffle[0][...], stack[...], preferred_element_type=f32).astype(bf16).reshape(count, slab, PIECE)
         )
 
     def unpack(got):
         stack[...] = jnp.dot(
-            shuffle[1], got[...].reshape(size, PIECE), preferred_element_type=f32
+            shuffle[1][...], got[...].reshape(size, PIECE), preferred_element_type=f32
         ).astype(bf16)
 
     def send_all(src, dst, ssem, rsem):
@@ -459,9 +389,6 @@
         early_out,
     )
     pl.semaphore_wait(barrier, count + 2)
-    near = remote(
-        own_in.at[pl.ds(0, near_in.shape[0])], near_in, near_send, near_recv, (weight_pair(x, e % cores), e)
-    )
     near.start()
     send_all(early_out, early_in, early_send, early_recv)
     pack(
@@ -588,6 +515,7 @@
         whole_context(s).wait_recv()
         parts[s - 1] = project(s)
         remote(parts.at[s - 1], columns.at[x], column_send, column_recv, ((x + 4 - s) % 4, e)).start()
+    weight_rest()
     done = remote(parts, columns.at[pl.ds(0, 3)], column_send, column_recv, ((x + 1) % 4, e))
     done.wait_recv()
     update = jnp.concatenate([columns[d] for d in range(4)], axis=1).astype(f32)
@@ -596,7 +524,6 @@
     scale = lax.rsqrt(jnp.mean(total * total, axis=-1, keepdims=True) + norm_eps)
     normed[...] = (total * scale).astype(bf16)
     done.wait_send()
-    near.wait()
     keys.wait_send()
     for s in range(1, 4):
         whole_context(s).wait_send()
@@ -604,33 +531,140 @@
     all_of(late_out, late_in, late_send, late_recv).wait_send()
 
 
-def attend(grid, sent, destination, lengths, expert_index, router_weights, stream_t, query, key_value, weight_t, own_in):
+def layer_kernel(
+    grid,
+    sent,
+    destination,
+    lengths,
+    expert_index,
+    router_weights,
+    stream_t,
+    query,
+    key_value,
+    weight_hbm,
+    own_in,
+    own_out,
+    result,
+    residual,
+    normed,
+    dispatch,
+    combine,
+    raw_in,
+    split,
+    raw_out,
+    *rest,
+):
+    buffers, (weight_sem, out_sem, own_sem, pair_send, pair_recv), sems = rest[:18], rest[18:23], rest[23:]
+    cores = grid[0]
+    x = lax.axis_index("dp")
+    e = lax.axis_index("expert")
+    pair = (weight_pair(x, e % cores), e)
+    columns = raw_in.shape[1]
+    late_rows = pl.ds(sent, columns - sent)
+
+    def to_pair(src, dst, i):
+        return pltpu.make_async_remote_copy(
+            src_ref=src,
+            dst_ref=dst,
+            send_sem=pair_send.at[i],
+            recv_sem=pair_recv.at[i],
+            device_id=pair,
+            device_id_type=pl.DeviceIdType.MESH,
+        )
+
+    near = to_pair(own_in.at[pl.ds(0, sent)], raw_in.at[1, pl.ds(0, sent)], 0)
+    weight_in = to_pair(own_in.at[late_rows], raw_in.at[1, late_rows], 1)
+    weight_out = to_pair(own_out, raw_out.at[1], 2)
+    load_out = pltpu.make_async_copy(own_out, raw_out.at[0], out_sem)
+    load_out.start()
+
+    def weight_rest():
+        weight_in.start()
+        weight_out.start()
+
+    size = buffers[0].shape[0] * buffers[0].shape[1]
+    height, depth = weight_hbm.shape
+    if height <= columns and depth <= raw_in.shape[2]:
+        weight_t = raw_in.at[0, pl.ds(0, height), pl.ds(0, depth)]
+    else:
+        weight_t = buffers[17]
+    shuffle = [split.at[pl.ds(0, size), pl.ds(i * size, size)] for i in range(2)]
+    stack = split.at[pl.ds(0, size), pl.ds(2 * size, PIECE)]
+    attention_kernel(
+        grid,
+        destination,
+        lengths,
+        expert_index,
+        router_weights,
+        stream_t,
+        query,
+        key_value,
+        weight_hbm,
+        near,
+        weight_rest,
+        residual,
+        normed,
+        dispatch,
+        combine,
+        weight_t,
+        shuffle,
+        stack,
+        *buffers[:9],
+        weight_sem,
+        *sems[:10],
+    )
+    expert_kernel(
+        grid,
+        dispatch,
+        normed,
+        residual,
+        combine,
+        near,
+        weight_in,
+        weight_out,
+        load_out,
+        own_in,
+        result,
+        raw_in,
+        split,
+        raw_out,
+        *buffers[9:17],
+        own_sem,
+        *sems[10:],
+    )
+
+
+def layer(grid, destination, lengths, expert_index, router_weights, stream_t, query, key_value, weight_t, own_in, own_out):
     rows = destination.shape[1]
     width = stream_t.shape[0]
     count = grid[0] * grid[1] * grid[2]
     slab = PIECES * (rows // count)
-    size = count * slab
     slots = rows * TOPK
+    capacity = slots // count
+    part = slots // 4
+    columns = own_in.shape[0]
+    units = columns // 2
+    padded = -(-units // 128) * 128
     vmem = pl.BlockSpec(memory_space=pltpu.VMEM)
     hbm = pl.BlockSpec(memory_space=pl.ANY)
     dma = pltpu.SemaphoreType.DMA
     slabs = pltpu.VMEM((count, slab, PIECE), bf16)
+    buffer = pltpu.VMEM((count, capacity, width), bf16)
     early_width = query.shape[1] + key_value.shape[1]
+    carved = weight_t.shape[0] <= columns and weight_t.shape[1] <= width
     return pl.pallas_call(
-        functools.partial(attention_kernel, grid),
-        out_shape=[
-            jax.ShapeDtypeStruct((rows, width), f32),
-            jax.ShapeDtypeStruct((rows, width), bf16),
-            jax.ShapeDtypeStruct((slots, rows), bf16),
-            jax.ShapeDtypeStruct((2, rows, slots), bf16),
-            jax.ShapeDtypeStruct((sent, width), bf16),
-        ],
-        in_specs=[vmem, pl.BlockSpec(memory_space=pltpu.SMEM)] + [vmem] * 5 + [hbm] * 2,
-        out_specs=[vmem] * 4 + [hbm],
+        functools.partial(layer_kernel, grid, max(columns // 32, 1) * 16),
+        out_shape=jax.ShapeDtypeStruct((rows, width), bf16),
+        in_specs=[vmem, pl.BlockSpec(memory_space=pltpu.SMEM)] + [vmem] * 5 + [hbm] * 3,
+        out_specs=vmem,
         scratch_shapes=[
-            pltpu.VMEM(weight_t.shape, bf16),
-            pltpu.VMEM((2, size, size), bf16),
-            pltpu.VMEM((size, PIECE), bf16),
+            pltpu.VMEM((rows, width), f32),
+            pltpu.VMEM((rows, width), bf16),
+            pltpu.VMEM((slots, rows), bf16),
+            pltpu.VMEM((2, rows, slots), bf16),
+            pltpu.VMEM((2, columns, width), bf16),
+            pltpu.VMEM((4 * padded, width), bf16),
+            pltpu.VMEM((2, units, width), bf16),
             slabs,
             slabs,
             slabs,
@@ -640,16 +674,27 @@
             pltpu.VMEM((4, KV_HEADS, rows, HEADS // KV_HEADS * HEAD_DIM), bf16),
             pltpu.VMEM((3, rows, width // 4), bf16),
             pltpu.VMEM((4, rows, width // 4), bf16),
+            buffer,
+            buffer,
+            buffer,
+            pltpu.VMEM((2 * part, width), bf16),
+            pltpu.VMEM((2, 2 * part, padded), bf16),
+            pltpu.VMEM((2, part, width), f32),
+            buffer,
+            buffer,
+            pltpu.VMEM((16, 128) if carved else weight_t.shape, bf16),
         ]
-        + [dma] * 9
+        + [dma, dma, dma, dma((3,)), dma((3,))]
+        + [dma] * 6
         + [dma((3,))] * 2
-        + [dma] * 2,
+        + [dma] * 2
+        + [dma((4,))] * 8,
         compiler_params=pltpu.CompilerParams(
             collective_id=2, has_side_effects=True, vmem_limit_bytes=60 << 20
         ),
-        cost_estimate=pl.CostEstimate(flops=5 << 30, bytes_accessed=8 << 20, transcendentals=0),
-        name="attend",
-    )(destination, lengths, expert_index, router_weights, stream_t, query, key_value, weight_t, own_in)
+        cost_estimate=pl.CostEstimate(flops=18 << 30, bytes_accessed=30 << 20, transcendentals=0),
+        name="layer",
+    )(destination, lengths, expert_index, router_weights, stream_t, query, key_value, weight_t, own_in, own_out)
 
 
 def on_device(
@@ -669,10 +714,8 @@
     cores, ys = 2, 4
     grid = (cores, ys, expert_count // (cores * ys))
     own_in = gate_up[0].T
-    sent = own_in.shape[0] * 5 // 128 * 16
-    residual, normed, dispatch, combine, near_in = attend(
+    scored = layer(
         grid,
-        sent,
         destination.reshape(1, row_count),
         lengths,
         expert_index[0].T,
@@ -682,8 +725,8 @@
         key_value_rows,
         out_weight.T,
         own_in,
+        down_weight[0],
     )
-    scored = experts(grid, dispatch, normed, residual, combine, own_in, near_in, down_weight[0])
     return scored.reshape(1, row_count, model_width)
 
 

time: 243 us -> 233 us (0.959)
  Pallas kernels: 239 us -> 230 us
    pallas_call x2 -> x1, Pallas kernels: 239 us -> 230 us  [layer(): pl.pallas_call(functools.partial(layer_kernel, grid, max(columns // 32, 1...]
where the time goes in v4:
time: 233 us; the launch traced here: 232 us
  Pallas kernels  230 us (99%)
    pallas_call x1, Pallas kernels, layer(): pl.pallas_call(functools.partial(layer_kernel, grid, max(columns // 32, 1...  230 us

profile of v4, /device:TPU:1, one launch (start us, length us, event | category | flops | bytes accessed | tf_op | source)
XLA Modules:
  0.0 232.1 jit_solution(686036390284269531)
XLA Ops:
  0.0 229.9 %layer.1 = bf16[128,2880]{1,0:T(8,128)(2,1)} custom-call(s32[1,128]{1,0:T(1,128)} %bitcast.21, s32[1,3]{1,0:T(1,128)} %lengths.1, s32[4,128]{1,0:T(4,128)} %bitcast.19, f32[4,128]{1,0:T(4,128)} %bitcast.20, bf16[2880,128]{1,0:T(8,128)(2,1)} %bitcast.18, bf16[128,2048]{1,0:T(8,128)(2,1)} %query.1, bf16[128,512]{1,0:T(8,128)(2,1)} %key_value.1, ...), custom_call_target="tpu_custom_call" | custom-call | flops 19327352832 | bytes 31457280 | tf_op jit(solution)/shard_map/layer/pallas_call | solution.py:655
  229.9 2.3 copy.11

commit v5 on v4

--- a/solution.py
+++ b/solution.py
@@ -229,31 +229,28 @@
     lax.fori_loop(0, 6, step, 0)
     ret_recv[0] = out_buf[0]
 
+    for c in range(4):
+        view = ret_recv.at[pl.ds(1, per - 1)] if c == 0 else chunk_of(ret_recv, c)
+        remote(view, view, go_send.at[0], ret_rsem.at[c], twin).wait_recv()
+        for start in range(0, width, 768):
+            size = min(768, width - start)
+            cols = pl.ds(start, size)
+            back = ret_recv[pl.ds(c * per, per), :, cols].reshape(rows, size)
+            mixed = residual[:, cols]
+            for i in range(2):
+                mixed += jnp.dot(combine[i, :, pl.ds(c * rows, rows)], back, preferred_element_type=f32)
+            if c < 3:
+                residual[:, cols] = mixed
+            else:
+                result[:, cols] = mixed.astype(bf16)
+
     def finish(c, carry):
         forward(c).wait_send()
         partial(c).wait_send()
         wait_sent(out_buf, ret_send, c)
-
-        @pl.when(c == 0)
-        def _():
-            view = ret_recv.at[pl.ds(1, per - 1)]
-            remote(view, view, go_send.at[0], ret_rsem.at[0], twin).wait_recv()
-
-        @pl.when(c > 0)
-        def _():
-            view = chunk_of(ret_recv, c)
-            remote(view, view, go_send.at[0], ret_rsem.at[c], twin).wait_recv()
-
         return carry
 
     lax.fori_loop(0, 4, finish, 0)
-    for start in range(0, width, 768):
-        size = min(768, width - start)
-        cols = pl.ds(start, size)
-        back = ret_recv[:, :, cols].reshape(slabs * capacity, size)
-        mixed = jnp.dot(combine[0], back, preferred_element_type=f32)
-        mixed += jnp.dot(combine[1], back, preferred_element_type=f32)
-        result[:, cols] = (residual[:, cols] + mixed).astype(bf16)
 
 
 PIECE = 384
@@ -332,8 +329,6 @@
     column = lax.broadcasted_iota(jnp.int32, (size, size), 1)
     source = (row % slab) // share * rows + row // slab * share + row % share
     shuffle[0][...] = (column == source).astype(f32).astype(bf16)
-    source = (row % rows) // share * slab + row // rows * share + row % share
-    shuffle[1][...] = (column == source).astype(f32).astype(bf16)
 
     def pack(values, out):
         stack[...] = jnp.zeros_like(stack)
@@ -403,6 +398,8 @@
         late_out,
     )
     send_all(late_out, late_in, late_send, late_recv)
+    source = (row % rows) // share * slab + row // rows * share + row % share
+    shuffle[1][...] = (column == source).astype(f32).astype(bf16)
 
     slots, capacity = dispatch.shape[0], dispatch.shape[0] // count
     holder = peer(e, lax.broadcasted_iota(jnp.int32, (count, 1), 0), 1, cores, ys, zs)
@@ -431,13 +428,19 @@
     last, offset = early_width // PIECE, early_width % PIECE
     spots = stack[pl.ds(last * rows, rows), pl.ds(offset, 128)].astype(f32)
     settle = jnp.transpose(spots)[:rows].astype(bf16)
-    for piece in range(last + 1):
+
+    def move_piece(piece):
         part = min(PIECE, early_width - piece * PIECE)
         moved = jnp.dot(settle, stack[pl.ds(piece * rows, rows), :], preferred_element_type=f32).astype(bf16)
         sorted_rows[:, pl.ds(piece * PIECE, part)] = moved[:, :part]
+
+    for piece in range(query_width // PIECE, last + 1):
+        move_piece(piece)
     section[0] = sorted_rows[:, pl.ds(query_width, memory_width)]
     for s in range(1, 4):
         remote(section.at[0], section.at[s], key_send, key_recv, ((x + s) % 4, e)).start()
+    for piece in range(query_width // PIECE):
+        move_piece(piece)
 
     keys = remote(section.at[pl.ds(1, 3)], section.at[pl.ds(1, 3)], key_send, key_recv, ((x + 1) % 4, e))
     keys.wait_recv()
@@ -515,9 +518,9 @@
         whole_context(s).wait_recv()
         parts[s - 1] = project(s)
         remote(parts.at[s - 1], columns.at[x], column_send, column_recv, ((x + 4 - s) % 4, e)).start()
-    weight_rest()
     done = remote(parts, columns.at[pl.ds(0, 3)], column_send, column_recv, ((x + 1) % 4, e))
     done.wait_recv()
+    weight_rest()
     update = jnp.concatenate([columns[d] for d in range(4)], axis=1).astype(f32)
     total = residual[...] + update
     residual[...] = total

time: 233 us -> 233 us (level)
  no operation moved by 1% of the time
where the time goes in v5:
time: 233 us; the launch traced here: 232 us
  Pallas kernels  230 us (99%)
    pallas_call x1, Pallas kernels, layer(): pl.pallas_call(functools.partial(layer_kernel, grid, max(columns // 32, 1...  230 us

profile of v5, /device:TPU:1, one launch (start us, length us, event | category | flops | bytes accessed | tf_op | source)
XLA Modules:
  0.0 232.5 jit_solution(18335032134436972870)
XLA Ops:
  0.0 230.2 %layer.1 = bf16[128,2880]{1,0:T(8,128)(2,1)} custom-call(s32[1,128]{1,0:T(1,128)} %bitcast.21, s32[1,3]{1,0:T(1,128)} %lengths.1, s32[4,128]{1,0:T(4,128)} %bitcast.19, f32[4,128]{1,0:T(4,128)} %bitcast.20, bf16[2880,128]{1,0:T(8,128)(2,1)} %bitcast.18, bf16[128,2048]{1,0:T(8,128)(2,1)} %query.1, bf16[128,512]{1,0:T(8,128)(2,1)} %key_value.1, ...), custom_call_target="tpu_custom_call" | custom-call | flops 19327352832 | bytes 31457280 | tf_op jit(solution)/shard_map/layer/pallas_call | solution.py:658
  230.2 2.3 copy.11

commit v6 on v5

--- a/solution.py
+++ b/solution.py
@@ -456,6 +456,22 @@
     key_place = (x + 4 - key_lane // rows) % 4 * rows + key_lane % rows
     query_place = x * rows + lax.broadcasted_iota(jnp.int32, (rows, key_count), 0)
     seen = ((segment(key_place) == segment(query_place)) & (key_place <= query_place))[None]
+    def context_piece(s, h):
+        near_by = s != 2
+        source = 0 if near_by else 1 + 2 * (h % 2)
+        step = s if near_by else source
+        return remote(
+            context.at[source, h],
+            context.at[s, h],
+            context_send.at[(s - 1) * KV_HEADS + h],
+            context_recv.at[(s - 1) * KV_HEADS + h],
+            ((x + step) % 4, e),
+        )
+
+    def pass_on(h):
+        context_piece(1 + 2 * (h % 2), h).wait_recv()
+        context_piece(2, h).start()
+
     for h in range(KV_HEADS):
         key = section[:, :, h * HEAD_DIM : (h + 1) * HEAD_DIM].reshape(key_count, HEAD_DIM)
         value = section[:, :, key_width + h * HEAD_DIM : key_width + (h + 1) * HEAD_DIM].reshape(
@@ -480,11 +496,13 @@
         ).reshape(group, rows, HEAD_DIM)
         heads = (numerator / denominator).astype(bf16)
         context[0, h] = jnp.concatenate([heads[g] for g in range(group)], axis=1)
-        for s in (2, 1, 3):
-            remote(
-                context.at[0, h], context.at[s, h], context_send.at[s - 1], context_recv.at[s - 1], ((x + s) % 4, e)
-            ).start()
-
+        for s in (1, 3):
+            context_piece(s, h).start()
+        if h >= 2:
+            pass_on(h - 2)
+
+    for h in range(KV_HEADS - 2, KV_HEADS):
+        pass_on(h)
     load.wait()
     depth = group * HEAD_DIM
 
@@ -500,11 +518,6 @@
             total = term if total is None else total + term
         return total.astype(bf16)
 
-    def whole_context(s):
-        return remote(
-            context.at[0], context.at[s], context_send.at[s - 1], context_recv.at[s - 1], ((x + s) % 4, e)
-        )
-
     columns[x] = project(0)
     all_of(late_out, late_in, late_send, late_recv).wait_recv()
     unpack(late_in)
@@ -515,7 +528,9 @@
         )
         residual[:, pl.ds(start, part)] = moved[:, :part]
     for s in (1, 3, 2):
-        whole_context(s).wait_recv()
+        for h in range(KV_HEADS):
+            if s != 1 + 2 * (h % 2):
+                context_piece(s, h).wait_recv()
         parts[s - 1] = project(s)
         remote(parts.at[s - 1], columns.at[x], column_send, column_recv, ((x + 4 - s) % 4, e)).start()
     done = remote(parts, columns.at[pl.ds(0, 3)], column_send, column_recv, ((x + 1) % 4, e))
@@ -529,7 +544,8 @@
     done.wait_send()
     keys.wait_send()
     for s in range(1, 4):
-        whole_context(s).wait_send()
+        for h in range(KV_HEADS):
+            context_piece(s, h).wait_send()
     all_of(early_out, early_in, early_send, early_recv).wait_send()
     all_of(late_out, late_in, late_send, late_recv).wait_send()
 
@@ -689,7 +705,7 @@
         ]
         + [dma, dma, dma, dma((3,)), dma((3,))]
         + [dma] * 6
-        + [dma((3,))] * 2
+        + [dma((3 * KV_HEADS,))] * 2
         + [dma] * 2
         + [dma((4,))] * 8,
         compiler_params=pltpu.CompilerParams(

time: 233 us -> 225 us (0.966)
  Pallas kernels: 230 us -> 222 us
    pallas_call x1, Pallas kernels: 230 us -> 222 us  [layer(): pl.pallas_call(functools.partial(layer_kernel, grid, max(columns // 32, 1...]
where the time goes in v6:
time: 225 us; the launch traced here: 224 us
  Pallas kernels  222 us (99%)
  local copies, waits for them, and re-layouts  2.26 us (1%)
    pallas_call x1, Pallas kernels, layer(): pl.pallas_call(functools.partial(layer_kernel, grid, max(columns // 32, 1...  222 us

profile of v6, /device:TPU:1, one launch (start us, length us, event | category | flops | bytes accessed | tf_op | source)
XLA Modules:
  0.0 224.1 jit_solution(17360873035345682890)
XLA Ops:
  0.0 221.8 %layer.1 = bf16[128,2880]{1,0:T(8,128)(2,1)} custom-call(s32[1,128]{1,0:T(1,128)} %bitcast.21, s32[1,3]{1,0:T(1,128)} %lengths.1, s32[4,128]{1,0:T(4,128)} %bitcast.19, f32[4,128]{1,0:T(4,128)} %bitcast.20, bf16[2880,128]{1,0:T(8,128)(2,1)} %bitcast.18, bf16[128,2048]{1,0:T(8,128)(2,1)} %query.1, bf16[128,512]{1,0:T(8,128)(2,1)} %key_value.1, ...), custom_call_target="tpu_custom_call" | custom-call | flops 19327352832 | bytes 31457280 | tf_op jit(solution)/shard_map/layer/pallas_call | solution.py:674
  221.8 2.3 %copy.11 = bf16[1,128,2880]{1,2,0:T(8,128)(2,1)} copy(bf16[1,128,2880]{2,1,0:T(8,128)(2,1)} %bitcast.14) | data formatting | bytes 1474560 | tf_op jit(solution)/shard_map/reshape | solution.py:749
